TPU v7x, 256 devices: a whole 4x4x8 slice. The times are simulated.
256 devices in a mesh: dp: 32 (over x, z), head: 8 (over y, core).
Axes of the slice: x: 4, y: 4, z: 8, core: 2. Of those that a mesh axis runs over, the one named last changes fastest.
Arguments:
- key_grads: bfloat16 [2, 16384, 2048], P(None, 'dp', 'head'), may hold values from -6 to 6
- value_grads: bfloat16 [2, 16384, 2048], P(None, 'dp', 'head'), may hold values from -6 to 6
- key_weight: bfloat16 [2, 3584, 2048], P(None, 'dp', 'head'), may hold values from -0.125 to 0.125
- value_weight: bfloat16 [2, 3584, 2048], P(None, 'dp', 'head'), may hold values from -0.125 to 0.125
- block_source: int32 [1024], replicated, may hold values from 0 to 1023, as said below
- hidden_mid: bfloat16 [16384, 3584], P('dp', 'head')
- mlp_out: bfloat16 [16384, 3584], P('dp', 'head')
- post_gain: bfloat16 [3584], P('head'), may hold values from 0.5 to 2
- final_gain: bfloat16 [3584], P('head'), may hold values from 0.5 to 2
- gate_pre: bfloat16 [16384, 7168], P('dp', 'head'), may hold values from -6 to 6
- up_pre: bfloat16 [16384, 7168], P('dp', 'head'), may hold values from -6 to 6
- down_weight: bfloat16 [7168, 3584], P('head', 'dp'), may hold values from -0.09375 to 0.09375
Outputs:
- resid_grad: bfloat16 [16384, 3584], P('dp', 'head')
- gate_grad: bfloat16 [16384, 7168], P('dp', 'head')
- up_grad: bfloat16 [16384, 7168], P('dp', 'head')
Inputs may be any that keep to these rules, and one draw needn't show every extreme that they name: block_source is a permutation of the 1024 row blocks. The decoder blocks of one device are blocks 32 * a to 32 * a + 31, and the encoder blocks of device b are blocks 32 * b to 32 * b + 31; at most 2 decoder blocks of one device fill encoder blocks of one device, and exactly 2 do for some pairs of devices in every draw.
All inputs are finite; a program needn't handle non-finite values.
Results may differ from a plain program's by a relative error of at most 0.02.
Values may be sent and summed in bfloat16 or wider, within the bound.
No kernel may reach another device: no remote copies, remote signals or barrier semaphores. Data moves between devices by JAX's collectives and lax.ppermute only.
A program may use at most 64 MiB of HBM per device.

v0:
```python
import jax
import jax.numpy as jnp
from jax import lax
from jax.experimental import pallas as pl
from jax.experimental.pallas import tpu as pltpu
from jax.sharding import PartitionSpec as P

EPS = 1e-06
NX, NZ, NY, NC = 4, 8, 4, 2
AXES = ("dp", "head")
BF = jnp.bfloat16
F32 = jnp.float32
MIB = 56


def move(value, dx=0, dz=0, dy=0, dc=0):
    pairs = []
    for x in range(NX):
        for z in range(NZ):
            for y in range(NY):
                for c in range(NC):
                    src = (x * NZ + z) * 8 + y * NC + c
                    dst = (
                        ((x + dx) % NX * NZ + (z + dz) % NZ) * 8
                        + (y + dy) % NY * NC
                        + (c + dc) % NC
                    )
                    pairs.append((src, dst))
    return lax.ppermute(value, AXES, pairs)


def spread_columns(shard):
    pairs = []
    for x in range(NX):
        for z in range(NZ):
            for y in range(NY):
                for c in range(NC):
                    d, t = z // 4, z % 4
                    src = (x * NZ + z) * 8 + y * NC + c
                    pairs.append((src, (t * NZ + 4 * c + x) * 8 + y * NC + d))
    return lax.ppermute(shard, AXES, pairs)


def call(kernel, out_shape, n_scalar, n_array, flops, scratch=(), name=None, space=pltpu.VMEM):
    return pl.pallas_call(
        kernel,
        out_shape=out_shape,
        in_specs=[pl.BlockSpec(memory_space=pltpu.SMEM)] * n_scalar
        + [pl.BlockSpec(memory_space=space)] * n_array,
        out_specs=jax.tree.map(lambda _: pl.BlockSpec(memory_space=pltpu.VMEM), out_shape),
        scratch_shapes=scratch,
        compiler_params=pltpu.CompilerParams(vmem_limit_bytes=MIB * 1024 * 1024),
        cost_estimate=pl.CostEstimate(flops=flops, bytes_accessed=6_000_000, transcendentals=0),
        name=name,
    )


def dot_nt(a, b):
    return lax.dot_general(a, b, (((1,), (1,)), ((), ())), preferred_element_type=F32)


def dot_tn(a, b):
    return lax.dot_general(a, b, (((0,), (0,)), ((), ())), preferred_element_type=F32)


def part_kernel(where, core, *refs):
    pieces, outs, (wall, rows, sems) = refs[:8], refs[-7:-3], refs[-3:]
    count = (len(refs) - 15) // 2
    copies = []
    for k, ref in enumerate(pieces):
        at = pl.multiple_of(where[k] % 4 * 112, 16)
        spot = wall.at[where[k] // 4, pl.ds(at, 112)]
        copies.append(pltpu.make_async_copy(ref, spot, sems.at[k]))
    at = 0
    for k in range(count):
        size = refs[8 + k].shape[0]
        for side in range(2):
            spot = rows.at[side, pl.ds(at, size)]
            ref, sem = refs[8 + side * count + k], sems.at[8 + 2 * k + side]
            copies.append(pltpu.make_async_copy(ref, spot, sem))
        at += size
    for copy in copies:
        copy.start()
    for copy in copies[:8]:
        copy.wait()
    own, other = wall[core[0]], wall[1 - core[0]]
    at = 0
    for k in range(count):
        size = refs[8 + k].shape[0]
        copies[8 + 2 * k].wait()
        copies[9 + 2 * k].wait()
        prod = dot_nt(own, rows[0, at : at + size, :])
        prod = (prod + dot_nt(other, rows[1, at : at + size, :])).astype(BF)
        for k in range(4):
            outs[k][:, at : at + size] = prod[k * 112 : (k + 1) * 112, :]
        at += size


def send_kernel(xs, *refs):
    first, last, (lane_pos, out, moved) = refs[:4], refs[4:8], refs[8:]
    for r in range(4):
        parts, at = (first, r * 512) if r < 3 else (last, 0)
        total = parts[0][:, at : at + 512].astype(F32)
        for part in parts[1:]:
            total = total + part[:, at : at + 512].astype(F32)
        ids = lax.broadcasted_iota(jnp.int32, (1024, 512), 0)
        pick = jnp.where(ids == lane_pos[r : r + 1, :], 1.0, 0.0).astype(BF)
        moved[xs[r]] = dot_nt(total.astype(BF), pick).astype(BF)
    group = lax.broadcasted_iota(jnp.int32, (112, 128), 1) // 32
    for q in range(8):
        tiles = [moved[x, :, q * 128 : (q + 1) * 128] for x in range(4)]
        for j in range(4):
            here = tiles[(0 - j) % 4]
            for g in range(1, 4):
                here = jnp.where(group == g, tiles[(g - j) % 4], here)
            out[4 * q + j] = here


def stats_kernel(bundle, stats, held, sems):
    copies = []
    for k in range(8):
        rows = bundle.at[pl.ds(k * 912, 912)]
        copies.append(pltpu.make_async_copy(rows, held.at[k], sems.at[k]))
    for copy in copies:
        copy.start()
    for copy in copies:
        copy.wait()

    def out_sum(k, total):
        value = held[k, 448:896, :].astype(F32)
        return total + jnp.sum(value * value, axis=0, keepdims=True)

    total = lax.fori_loop(0, 8, out_sum, jnp.zeros((1, 512), F32))
    out_scale = lax.rsqrt(total / 3584.0 + EPS)

    def resid_sums(k, sums):
        gain = held[k, 896:912, :].astype(F32).T[:448, 0:1]
        gout = held[k, 448:896, :].astype(F32) * gain
        resid = held[k, 0:448, :].astype(F32) + gout * out_scale
        square = jnp.sum(resid * resid, axis=0, keepdims=True)
        return sums[0] + square, sums[1] + jnp.sum(resid * gout, axis=0, keepdims=True)

    zero = jnp.zeros((1, 512), F32)
    square, cross = lax.fori_loop(0, 8, resid_sums, (zero, zero))
    stats[...] = jnp.concatenate(
        [out_scale, lax.rsqrt(square / 3584.0 + EPS), cross, jnp.zeros((5, 512), F32)], axis=0
    )


def recv_kernel(arrived, row_pos, mid, out, gain_post, gain_final, stats, grad):
    ids = lax.broadcasted_iota(jnp.int32, (1024, 512), 0)
    pick = jnp.where(ids == row_pos[...], 1.0, 0.0).astype(BF)
    out_scale = stats[0:1, :]
    first = jnp.zeros((1, 512), F32)
    second = jnp.zeros((1, 512), F32)
    for x in range(4):
        side = jnp.concatenate([arrived[x * 8 + z] for z in range(8)], axis=1)
        rows = slice(x * 112, (x + 1) * 112)
        piece = jnp.dot(side, pick, preferred_element_type=F32)
        grad[rows, :] = piece.astype(BF)
        piece = piece * gain_final[rows, :]
        gout = out[rows, :].astype(F32) * gain_post[rows, :]
        resid = mid[rows, :].astype(F32) + gout * out_scale
        first = first + jnp.sum(piece * resid, axis=0, keepdims=True)
        second = second + jnp.sum(piece * gout, axis=0, keepdims=True)
    parts = []
    for value in (first, second):
        for _ in range(3):
            parts.append(value.astype(BF).astype(F32))
            value = value - parts[-1]
    parts.append(jnp.zeros((10, 512), F32))
    grad[448:464, :] = jnp.concatenate(parts, axis=0).astype(BF)


def row_factors(stats, grads):
    sums = grads[0, 448:464, :].astype(F32)
    for k in range(1, 8):
        sums = sums + grads[k, 448:464, :].astype(F32)
    first = sums[0:1, :] + sums[1:2, :] + sums[2:3, :]
    second = sums[3:4, :] + sums[4:5, :] + sums[5:6, :]
    out_scale, resid_scale, cross = stats[0:1, :], stats[1:2, :], stats[2:3, :]
    final_mean = resid_scale * first / 3584.0
    post_dot = resid_scale * (second - resid_scale * final_mean * cross)
    post_mean = out_scale * post_dot / 3584.0
    return out_scale, resid_scale, resid_scale * final_mean, out_scale * post_mean


def final_kernel(heads, *refs):
    grads, (weight, bundle, slope, active, stats, resid_grad, gate, up) = refs[:8], refs[8:16]
    grad_buf, weight_buf, held, scale_buf, stat_buf, value, sems = refs[16:]
    copies = [pltpu.make_async_copy(stats, stat_buf, sems.at[26])]
    for k in range(8):
        copies.append(pltpu.make_async_copy(grads[k], grad_buf.at[k], sems.at[k]))
    for k in range(8):
        at = pl.multiple_of(heads[k] * 448, 64)
        start = pl.multiple_of(heads[k] * 912, 16)
        rows = bundle.at[pl.ds(start, 912)]
        copies.append(pltpu.make_async_copy(rows, held.at[k], sems.at[8 + k]))
        rows = weight.at[pl.ds(at, 448)]
        copies.append(pltpu.make_async_copy(rows, weight_buf.at[k], sems.at[16 + k]))
    copies.append(pltpu.make_async_copy(slope, scale_buf.at[0], sems.at[24]))
    copies.append(pltpu.make_async_copy(active, scale_buf.at[1], sems.at[25]))
    for copy in copies:
        copy.start()
    for copy in copies[:9]:
        copy.wait()
    out_scale, resid_scale, pull, push = row_factors(stat_buf, grad_buf)
    value[...] = jnp.zeros((512, 896), F32)

    @pl.loop(0, 8)
    def _(k):
        pltpu.make_async_copy(bundle.at[pl.ds(0, 912)], held.at[k], sems.at[8 + k]).wait()
        pltpu.make_async_copy(weight.at[pl.ds(0, 448)], weight_buf.at[k], sems.at[16 + k]).wait()
        gains = held[k, 896:912, :].astype(F32).T
        gain_post, gain_final = gains[:448, 0:1], gains[:448, 1:2]
        out = held[k, 448:896, :].astype(F32)
        resid = held[k, 0:448, :].astype(F32) + out * gain_post * out_scale
        norm_grad = grad_buf[k, 0:448, :].astype(F32) * gain_final
        total = resid_scale * (norm_grad - resid * pull)

        @pl.when(k == 0)
        def _():
            resid_grad[...] = total.astype(BF)

        post = out_scale * (total * gain_post - out * push)
        value[...] += dot_tn(post.astype(BF), weight_buf[k])

    for copy in copies[25:]:
        copy.wait()
    gate[...] = (value[...] * scale_buf[0]).astype(BF)
    up[...] = (value[...] * scale_buf[1]).astype(BF)


def gelu_parts(gate_value):
    activated, pullback = jax.vjp(
        lambda pre_act: jax.nn.gelu(pre_act, approximate=True), gate_value
    )
    return (activated, pullback(jnp.ones_like(gate_value))[0])


def per_device(
    key_grads,
    value_grads,
    key_weight,
    value_weight,
    block_source,
    hidden_mid,
    mlp_out,
    post_gain,
    final_gain,
    gate_pre,
    up_pre,
    down_weight,
):
    dev = lax.axis_index("dp")
    head = lax.axis_index("head")
    x, z = dev // NZ, dev % NZ
    y, c = head // NC, head % NC

    weight = jnp.concatenate([key_weight[0], key_weight[1], value_weight[0], value_weight[1]], 1)
    weight, key_grads, value_grads = lax.optimization_barrier((weight, key_grads, value_grads))
    rows = jnp.concatenate([key_grads[0], key_grads[1], value_grads[0], value_grads[1]], 1)
    block_ids = jnp.arange(1024, dtype=jnp.int32)
    is_source = block_source[:, None] == block_ids[None, :]
    dest_block = jnp.sum(jnp.where(is_source, block_ids[:, None], 0), axis=0)
    dest_device = (dest_block // 32).reshape(32, 32)
    same_dest = dest_device[:, :, None] == dest_device[:, None, :]
    slot_ids = jnp.arange(32, dtype=jnp.int32)
    before = slot_ids[None, :] < slot_ids[:, None]
    rank = jnp.sum((same_dest & before[None]).astype(jnp.int32), axis=2)
    own_x = jnp.stack([x, (x + 3) % 4, (x + 1) % 4, (x + 2) % 4]).astype(jnp.int32)
    spread_ids = (own_x * NZ + z)[:, None, None] == slot_ids[None, :, None]
    dest_own = jnp.sum(jnp.where(spread_ids, dest_device[None], 0), axis=1)
    rank_own = jnp.sum(jnp.where(spread_ids, rank[None], 0), axis=1)
    lanes = (
        (dest_own // 4) * 128 + ((dest_own % 4 + own_x[:, None]) % 4) * 32 + rank_own * 16
    )
    lane_pos = (lanes[:, :, None] + jnp.arange(16, dtype=jnp.int32)).reshape(4, 512)
    source = lax.dynamic_slice_in_dim(block_source, dev * 32, 32)
    source_dev = source // 32
    source_rank = jnp.sum(
        jnp.where(block_ids[None, :] == source[:, None], rank.reshape(-1)[None, :], 0), axis=1
    )
    spot = (
        (source_dev % NZ) * 128 + ((dev % 4 + source_dev // NZ) % 4) * 32 + source_rank * 16
    )
    row_pos = (spot[:, None] + jnp.arange(16, dtype=jnp.int32)).reshape(1, 512)

    where = ((z - jnp.array([0, 1, 2, 3, 4, -1, -2, -3], jnp.int32)) % NZ).astype(jnp.int32)
    core = c.reshape(1).astype(jnp.int32)

    w0 = spread_columns(weight)
    s0 = move(rows, dc=1)
    gains = jnp.pad(jnp.stack([post_gain, final_gain]), ((0, 14), (0, 64)))
    bundle = jnp.concatenate([hidden_mid.T, mlp_out.T, gains], axis=0)
    bundle = lax.all_gather(bundle, "head", axis=0, tiled=True)
    w0, where = lax.optimization_barrier((w0, where))
    r1, r2 = move(rows, dx=1), move(rows, dx=-1)
    f1, g1 = move(w0, dz=1), move(w0, dz=-1)
    f2, g2 = move(f1, dz=1), move(g1, dz=-1)
    r1, r2, f2, g2, s0 = lax.optimization_barrier((r1, r2, f2, g2, s0))
    f3, g3 = move(f2, dz=1), move(g2, dz=-1)
    f4 = move(f3, dz=1)
    s1, s2 = move(r1, dc=1), move(r2, dc=1)
    r3 = move(r1, dx=1)

    gain_post = post_gain.astype(F32)[:, None]
    gain_final = final_gain.astype(F32)[:, None]
    active, slope = gelu_parts(gate_pre.astype(F32))
    slope = slope * up_pre.astype(F32)
    down_share, r1 = lax.optimization_barrier((down_weight.T, r1))
    down = lax.all_gather(down_share, "dp", axis=0, tiled=True)

    pieces = (w0, f1, f2, f3, f4, g1, g2, g3)

    place = (where // 4 * 4 + (where % 4 - y) % NY).astype(jnp.int32)

    def part(left, right):
        size = sum(ref.shape[0] for ref in left)
        parts = call(
            part_kernel,
            (jax.ShapeDtypeStruct((112, size), BF),) * 4,
            2,
            8 + 2 * len(left),
            2 * size * 448 * 2048,
            [
                pltpu.VMEM((2, 448, 1024), BF),
                pltpu.VMEM((2, size, 1024), BF),
                pltpu.SemaphoreType.DMA((8 + 2 * len(left),)),
            ],
            name="part",
            space=pl.ANY,
        )(place, core, *pieces, *left, *right)
        return parts

    def over_y(parts):
        return [parts[0]] + [move(parts[k], dy=k) for k in (2, 1, 3)]

    first = part((rows, r1, r2), (s0, s1, s2))
    first, r3 = lax.optimization_barrier((first, r3))
    last = part((r3,), (move(r3, dc=1),))
    groups = over_y(first) + over_y(last)
    groups[0], lane_pos, row_pos = lax.optimization_barrier((groups[0], lane_pos, row_pos))
    outgoing = call(
        send_kernel,
        jax.ShapeDtypeStruct((32, 112, 128), BF),
        1,
        len(groups) + 1,
        2 * 112 * 2048 * 1024,
        [pltpu.VMEM((4, 112, 1024), BF)],
        name="send",
    )(own_x, *groups, lane_pos)
    arrived = lax.all_to_all(outgoing, "dp", 0, 0, tiled=True)
    stats = call(
        stats_kernel,
        jax.ShapeDtypeStruct((8, 512), F32),
        0,
        1,
        3584 * 512 * 12,
        [pltpu.VMEM((8, 912, 512), BF), pltpu.SemaphoreType.DMA((8,))],
        name="stats",
        space=pl.ANY,
    )(bundle)
    arrived, stats, active, slope = lax.optimization_barrier((arrived, stats, active, slope))
    mid, out = hidden_mid.T, mlp_out.T
    grad = call(
        recv_kernel,
        jax.ShapeDtypeStruct((464, 512), BF),
        0,
        7,
        2 * 448 * 512 * 1024,
        name="recv",
    )(arrived, row_pos, mid, out, gain_post, gain_final, stats)
    p1, p2, p3 = move(grad, dy=1), move(grad, dy=-1), move(grad, dy=2)
    q0 = move(grad, dc=1)
    q1, q2, q3 = move(p1, dc=1), move(p2, dc=1), move(p3, dc=1)
    from_y = jnp.stack([y, y, y + 3, y + 3, y + 1, y + 1, y + 2, y + 2]) % 4
    from_c = (c + jnp.array([0, 1] * 4, jnp.int32)) % 2
    heads = (from_y * 2 + from_c).astype(jnp.int32)
    resid_grad, gate_grad, up_grad = call(
        final_kernel,
        (
            jax.ShapeDtypeStruct((448, 512), BF),
            jax.ShapeDtypeStruct((512, 896), BF),
            jax.ShapeDtypeStruct((512, 896), BF),
        ),
        1,
        13,
        2 * 512 * 896 * 3584,
        [
            pltpu.VMEM((8, 464, 512), BF),
            pltpu.VMEM((8, 448, 896), BF),
            pltpu.VMEM((8, 912, 512), BF),
            pltpu.VMEM((2, 512, 896), F32),
            pltpu.VMEM((8, 512), F32),
            pltpu.VMEM((512, 896), F32),
            pltpu.SemaphoreType.DMA((27,)),
        ],
        name="final",
        space=pl.ANY,
    )(heads, grad, q0, p1, q1, p2, q2, p3, q3, down, bundle, slope, active, stats)
    return (resid_grad.T, gate_grad, up_grad)


def solution(mesh):
    return jax.shard_map(
        per_device,
        mesh=mesh,
        in_specs=(
            P(None, "dp", "head"),
            P(None, "dp", "head"),
            P(None, "dp", "head"),
            P(None, "dp", "head"),
            P(),
            P("dp", "head"),
            P("dp", "head"),
            P("head"),
            P("head"),
            P("dp", "head"),
            P("dp", "head"),
            P("head", "dp"),
        ),
        out_specs=(P("dp", "head"), P("dp", "head"), P("dp", "head")),
        check_vma=False,
    )
```

profile of v0, /device:TPU:33, one launch (start us, length us, event | category | flops | bytes accessed | tf_op | source)
XLA Modules:
  0.0 205.2 jit_solution(7242361837138291728)
XLA Ops:
  8.7 2.2 %pad_maximum_fusion.1 = bf16[912,512]{1,0:T(8,128)(2,1)} fusion(bf16[16,512]{1,0:T(8,128)(2,1)S(1)} %fusion.14, bf16[448,512]{1,0:T(8,128)(2,1)} %bitcast.33, bf16[448,512]{1,0:T(8,128)(2,1)} %bitcast.31), kind=kLoop, calls=%fused_computation.16 | loop fusion | flops 2801664 | bytes 1867776 | tf_op jit(solution)/shard_map/concatenate | solution.py:295
  11.1 0.8 copy-done.7
  12.1 1.3 collective-permute-start.2
  13.4 1.5 collective-permute-start.3
  14.9 1.2 collective-permute-start.7
  16.1 7.1 %collective-permute-start = (bf16[112,1024]{1,0:T(8,128)(2,1)S(1)}, bf16[112,1024]{1,0:T(8,128)(2,1)S(1)}, u32[]{:S(2)}, u32[]{:S(2)}) collective-permute-start(bf16[112,1024]{1,0:T(8,128)(2,1)S(1)} %pad_maximum_fusion.2), channel_id=1, source_target_pairs={{0,0},{1,32},{2,2},{3,34},{4,4},{5,36},{6,6},{7,38},{8,64},{9,96},... | collective-permute-start | bytes 688136 | tf_op jit(solution)/shard_map/ppermute | solution.py:41
  23.2 9.0 %collective-permute-done.refs_0_ = bf16[112,1024]{1,0:T(8,128)(2,1)S(1)} collective-permute-done((bf16[112,1024]{1,0:T(8,128)(2,1)S(1)}, bf16[112,1024]{1,0:T(8,128)(2,1)S(1)}, u32[]{:S(2)}, u32[]{:S(2)}) %collective-permute-start) | collective-permute-done | bytes 229408 | tf_op jit(solution)/shard_map/ppermute | solution.py:41
  32.7 0.9 collective-permute-start.5
  33.6 3.8 %collective-permute-done.1.refs_1_ = bf16[112,1024]{1,0:T(8,128)(2,1)S(1)} collective-permute-done((bf16[112,1024]{1,0:T(8,128)(2,1)S(1)}, bf16[112,1024]{1,0:T(8,128)(2,1)S(1)}, u32[]{:S(2)}, u32[]{:S(2)}) %collective-permute-start.1) | collective-permute-done | bytes 229408 | tf_op jit(solution)/shard_map/ppermute | solution.py:29
  37.4 3.9 %collective-permute-start.4 = (bf16[112,1024]{1,0:T(8,128)(2,1)S(1)}, bf16[112,1024]{1,0:T(8,128)(2,1)S(1)}, u32[]{:S(2)}, u32[]{:S(2)}) collective-permute-start(bf16[112,1024]{1,0:T(8,128)(2,1)S(1)} %collective-permute-done.1.refs_1_), channel_id=1, source_target_pairs={{0,8},{1,9},{2,10},{3,11},{4,12},{5,13},{6,14},{7,15},{8,16},{9,17... | collective-permute-start | bytes 688136 | tf_op jit(solution)/shard_map/ppermute | solution.py:29
  41.3 2.0 collective-permute-done.5.refs_5_
  43.3 2.5 %collective-permute-done.4.refs_2_ = bf16[112,1024]{1,0:T(8,128)(2,1)S(1)} collective-permute-done((bf16[112,1024]{1,0:T(8,128)(2,1)S(1)}, bf16[112,1024]{1,0:T(8,128)(2,1)S(1)}, u32[]{:S(2)}, u32[]{:S(2)}) %collective-permute-start.4) | collective-permute-done | bytes 229408 | tf_op jit(solution)/shard_map/ppermute | solution.py:29
  45.9 4.0 %collective-permute-done.6.refs_6_ = bf16[112,1024]{1,0:T(8,128)(2,1)S(1)} collective-permute-done((bf16[112,1024]{1,0:T(8,128)(2,1)S(1)}, bf16[112,1024]{1,0:T(8,128)(2,1)S(1)}, u32[]{:S(2)}, u32[]{:S(2)}) %collective-permute-start.6) | collective-permute-done | bytes 229408 | tf_op jit(solution)/shard_map/ppermute | solution.py:29
  50.0 1.5 collective-permute-start.11
  52.3 1.5 collective-permute-start.8
  54.7 4.5 %collective-permute-done.8.refs_3_ = bf16[112,1024]{1,0:T(8,128)(2,1)} collective-permute-done((bf16[112,1024]{1,0:T(8,128)(2,1)S(1)}, bf16[112,1024]{1,0:T(8,128)(2,1)}, u32[]{:S(2)}, u32[]{:S(2)}) %collective-permute-start.8) | collective-permute-done | bytes 229408 | tf_op jit(solution)/shard_map/ppermute | solution.py:29
  59.3 1.4 collective-permute-start.9
  61.5 0.9 collective-permute-done.10.refs_7_
  62.4 3.0 %collective-permute-done.9.refs_4_ = bf16[112,1024]{1,0:T(8,128)(2,1)} collective-permute-done((bf16[112,1024]{1,0:T(8,128)(2,1)}, bf16[112,1024]{1,0:T(8,128)(2,1)}, u32[]{:S(2)}, u32[]{:S(2)}) %collective-permute-start.9) | collective-permute-done | bytes 229408 | tf_op jit(solution)/shard_map/ppermute | solution.py:29
  65.5 7.5 %part.2 = (bf16[112,1536]{1,0:T(8,128)(2,1)}, bf16[112,1536]{1,0:T(8,128)(2,1)}, bf16[112,1536]{1,0:T(8,128)(2,1)}, bf16[112,1536]{1,0:T(8,128)(2,1)}) custom-call(s32[8]{0:T(128)} %fusion.25.where, s32[1]{0:T(128)} %bitcast.12.core, bf16[112,1024]{1,0:T(8,128)(2,1)} %copy-done.18, bf16[112,1024]{1,0:T(8,128)(2,1)} %copy-done.19, ...), custom_call_target="tpu_custom_call" | custom-call | flops 2818572288 | bytes 6000000 | tf_op jit(solution)/shard_map/part/pallas_call | solution.py:320
  73.0 5.0 %collective-permute-done.13.refs_8_ = bf16[512,1024]{1,0:T(8,128)(2,1)S(1)} collective-permute-done((bf16[512,1024]{1,0:T(8,128)(2,1)}, bf16[512,1024]{1,0:T(8,128)(2,1)S(1)}, u32[]{:S(2)}, u32[]{:S(2)}) %collective-permute-start.13) | collective-permute-done | bytes 1048608 | tf_op jit(solution)/shard_map/ppermute | solution.py:29
  78.0 1.2 collective-permute-start.17
  79.6 2.9 %collective-permute-start.14 = (bf16[112,1536]{1,0:T(8,128)(2,1)}, bf16[112,1536]{1,0:T(8,128)(2,1)S(1)}, u32[]{:S(2)}, u32[]{:S(2)}) collective-permute-start(bf16[112,1536]{1,0:T(8,128)(2,1)} %get-tuple-element.55), channel_id=1, source_target_pairs={{0,4},{1,5},{2,6},{3,7},{4,0},{5,1},{6,2},{7,3},{8,12},{9,13},{10,... | collective-permute-start | bytes 1032200 | tf_op jit(solution)/shard_map/ppermute | solution.py:29
  83.1 2.3 %collective-permute-start.16 = (bf16[112,1536]{1,0:T(8,128)(2,1)}, bf16[112,1536]{1,0:T(8,128)(2,1)S(1)}, u32[]{:S(2)}, u32[]{:S(2)}) collective-permute-start(bf16[112,1536]{1,0:T(8,128)(2,1)} %get-tuple-element.57), channel_id=1, source_target_pairs={{0,6},{1,7},{2,0},{3,1},{4,2},{5,3},{6,4},{7,5},{8,14},{9,15},{10,... | collective-permute-start | bytes 1032200 | tf_op jit(solution)/shard_map/ppermute | solution.py:29
  86.4 1.0 copy-done.2
  87.4 4.9 %part.3 = (bf16[112,512]{1,0:T(8,128)(2,1)}, bf16[112,512]{1,0:T(8,128)(2,1)}, bf16[112,512]{1,0:T(8,128)(2,1)}, bf16[112,512]{1,0:T(8,128)(2,1)}) custom-call(s32[8]{0:T(128)} %fusion.25.where, s32[1]{0:T(128)} %bitcast.12.core, bf16[112,1024]{1,0:T(8,128)(2,1)} %copy-done.18, bf16[112,1024]{1,0:T(8,128)(2,1)} %copy-done.19, bf16[112,1024]{1,0:T(8,128)(2,1)} %copy-done.21, ...), custom_call_target="tpu_custom_call" | custom-call | flops 939524096 | bytes 6000000 | tf_op jit(solution)/shard_map/part/pallas_call | solution.py:320
  93.0 2.2 %collective-permute-start.20 = (bf16[112,512]{1,0:T(8,128)(2,1)}, bf16[112,512]{1,0:T(8,128)(2,1)S(1)}, u32[]{:S(2)}, u32[]{:S(2)}) collective-permute-start(bf16[112,512]{1,0:T(8,128)(2,1)} %get-tuple-element.62), channel_id=1, source_target_pairs={{0,6},{1,7},{2,0},{3,1},{4,2},{5,3},{6,4},{7,5},{8,14},{9,15},{10,... | collective-permute-start | bytes 344072 | tf_op jit(solution)/shard_map/ppermute | solution.py:29
  95.8 3.2 %collective-permute-done.15.refs_2_ = bf16[112,1536]{1,0:T(8,128)(2,1)S(1)} collective-permute-done((bf16[112,1536]{1,0:T(8,128)(2,1)}, bf16[112,1536]{1,0:T(8,128)(2,1)S(1)}, u32[]{:S(2)}, u32[]{:S(2)}) %collective-permute-start.15) | collective-permute-done | bytes 344096 | tf_op jit(solution)/shard_map/ppermute | solution.py:29
  99.0 1.9 collective-permute-done.18.refs_5_
  100.9 2.7 %collective-permute-done.19.refs_6_ = bf16[112,512]{1,0:T(8,128)(2,1)S(1)} collective-permute-done((bf16[112,512]{1,0:T(8,128)(2,1)}, bf16[112,512]{1,0:T(8,128)(2,1)S(1)}, u32[]{:S(2)}, u32[]{:S(2)}) %collective-permute-start.19) | collective-permute-done | bytes 114720 | tf_op jit(solution)/shard_map/ppermute | solution.py:29
  104.4 4.3 %send.1 = bf16[32,112,128]{2,1,0:T(8,128)(2,1)} custom-call(s32[4]{0:T(128)} %copy-done.28, bf16[112,1536]{1,0:T(8,128)(2,1)} %get-tuple-element.54.refs_0_, bf16[112,1536]{1,0:T(8,128)(2,1)} %copy-done.15, bf16[112,1536]{1,0:T(8,128)(2,1)} %copy-done.16, bf16[112,1536]{1,0:T(8,128)(2,1)} %copy-done.17, bf16[112,512]{1,0:T(8,128)(2,1)} %get-tuple-element.59.refs_4_, ...), custom_call_target="tpu_custom_call" | custom-call | flops 469762048 | bytes 6000000 | tf_op jit(solution)/shard_map/send/pallas_call | solution.py:344
  108.6 6.8 %all-to-all-start = ((bf16[32,112,128]{2,1,0:T(8,128)(2,1)}), bf16[32,112,128]{2,1,0:T(8,128)(2,1)S(1)}, u32[]{:S(2)}, u32[]{:S(2)}) async-start(bf16[32,112,128]{2,1,0:T(8,128)(2,1)} %send.1), calls=%async_computation | async-start | bytes 1835008 | tf_op jit(solution)/shard_map/all_to_all | solution.py:353
  115.5 0.8 copy.19.gain_post
  116.3 0.8 copy.20.gain_final
  117.2 3.1 %fusion.3 = (f32[512,896]{1,0:T(8,128)}, f32[512,896]{1,0:T(8,128)}) fusion(bf16[512,896]{1,0:T(8,128)(2,1)S(1)} %copy-done.4, bf16[512,896]{1,0:T(8,128)(2,1)S(1)} %copy-done.5), kind=kLoop, calls=%fused_computation.10 | loop fusion | flops 9633792 | bytes 5505024 | tf_op jit(solution)/shard_map/mul | solution.py:310
  120.3 7.6 %stats.1.refs_12_ = f32[8,512]{1,0:T(8,128)} custom-call(bf16[7296,512]{1,0:T(8,128)(2,1)} %all-gather.3.cloned.1.call-done.bundle.refs_9_), custom_call_target="tpu_custom_call" | custom-call | flops 22020096 | bytes 6000000 | tf_op jit(solution)/shard_map/stats/pallas_call | solution.py:354
  127.9 22.2 %all-to-all-done.arrived = bf16[32,112,128]{2,1,0:T(8,128)(2,1)S(1)} async-done(((bf16[32,112,128]{2,1,0:T(8,128)(2,1)}), bf16[32,112,128]{2,1,0:T(8,128)(2,1)S(1)}, u32[]{:S(2)}, u32[]{:S(2)}) %all-to-all-start) | async-done | bytes 917536 | tf_op jit(solution)/shard_map/all_to_all | solution.py:353
  150.2 0.9 copy-done
  151.1 3.3 %recv.1.refs_0_ = bf16[464,512]{1,0:T(8,128)(2,1)} custom-call(bf16[32,112,128]{2,1,0:T(8,128)(2,1)} %copy-done, s32[1,512]{1,0:T(1,128)} %add.273.row_pos, bf16[448,512]{1,0:T(8,128)(2,1)} %bitcast.32, bf16[448,512]{1,0:T(8,128)(2,1)} %bitcast.34, f32[448,1]{1,0:T(8,128)} %copy.19.gain_post, f32[448,1]{1,0:T(8,128)} %copy.20.gain_final, f32[8,512]{1,0:T(8,128)} %stats.1.refs_12_), custom_call_target="tpu_custom_call" | custom-call | flops 469762048 | bytes 6000000 | tf_op jit(solution)/shard_map/recv/pallas_call | solution.py:366
  154.4 1.2 collective-permute-start.22
  155.6 1.5 collective-permute-start.24
  157.1 1.2 collective-permute-start.26
  158.3 2.4 %collective-permute-start.21 = (bf16[464,512]{1,0:T(8,128)(2,1)}, bf16[464,512]{1,0:T(8,128)(2,1)S(1)}, u32[]{:S(2)}, u32[]{:S(2)}) collective-permute-start(bf16[464,512]{1,0:T(8,128)(2,1)} %recv.1.refs_0_), channel_id=1, source_target_pairs={{0,1},{1,0},{2,3},{3,2},{4,5},{5,4},{6,7},{7,6},{8,9},{9,8},{10,11... | collective-permute-start | bytes 1425416 | tf_op jit(solution)/shard_map/ppermute | solution.py:29
  160.7 5.3 %collective-permute-done.22.refs_2_ = bf16[464,512]{1,0:T(8,128)(2,1)S(1)} collective-permute-done((bf16[464,512]{1,0:T(8,128)(2,1)}, bf16[464,512]{1,0:T(8,128)(2,1)S(1)}, u32[]{:S(2)}, u32[]{:S(2)}) %collective-permute-start.22) | collective-permute-done | bytes 475168 | tf_op jit(solution)/shard_map/ppermute | solution.py:29
  166.0 4.3 %collective-permute-start.23 = (bf16[464,512]{1,0:T(8,128)(2,1)S(1)}, bf16[464,512]{1,0:T(8,128)(2,1)S(1)}, u32[]{:S(2)}, u32[]{:S(2)}) collective-permute-start(bf16[464,512]{1,0:T(8,128)(2,1)S(1)} %collective-permute-done.22.refs_2_), channel_id=1, source_target_pairs={{0,1},{1,0},{2,3},{3,2},{4,5},{5,4},{6,7},{7,6},{8,9},{9,8},{10,11... | collective-permute-start | bytes 1425416 | tf_op jit(solution)/shard_map/ppermute | solution.py:29
  170.4 8.4 %collective-permute-start.25 = (bf16[464,512]{1,0:T(8,128)(2,1)S(1)}, bf16[464,512]{1,0:T(8,128)(2,1)S(1)}, u32[]{:S(2)}, u32[]{:S(2)}) collective-permute-start(bf16[464,512]{1,0:T(8,128)(2,1)S(1)} %collective-permute-done.24.refs_4_), channel_id=1, source_target_pairs={{0,1},{1,0},{2,3},{3,2},{4,5},{5,4},{6,7},{7,6},{8,9},{9,8},{10,11... | collective-permute-start | bytes 1425416 | tf_op jit(solution)/shard_map/ppermute | solution.py:29
  178.7 1.8 collective-permute-start.27
  183.1 15.2 %final.1 = (bf16[448,512]{1,0:T(8,128)(2,1)}, bf16[512,896]{1,0:T(8,128)(2,1)}, bf16[512,896]{1,0:T(8,128)(2,1)}) custom-call(s32[8]{0:T(128)} %fusion.24.heads, bf16[464,512]{1,0:T(8,128)(2,1)} %recv.1.refs_0_, bf16[464,512]{1,0:T(8,128)(2,1)} %copy-done.11, bf16[464,512]{1,0:T(8,128)(2,1)} %copy-done.8, bf16[464,512]{1,0:T(8,128)(2,1)} %copy-done.12, ...), custom_call_target="tpu_custom_call" | custom-call | flops 3288334336 | bytes 6000000 | tf_op jit(solution)/shard_map/final/pallas_call | solution.py:380
  (130 shorter events, 11.4 us)
Async XLA Ops:
  7.2 113.1 %all-gather.3.cloned.1.call-start = ((), (), s32[]{:S(2)}) async-start(), calls=%async_computation.1 | async-start | bytes 8404992 | tf_op jit(solution)/shard_map/all_gather | solution.py:296
  10.9 170.3 %all-gather.5.cloned.1.call-start = ((), (), s32[]{:S(2)}) async-start(), calls=%async_computation.2 | async-start | bytes 6623232 | tf_op jit(solution)/shard_map/all_gather | solution.py:312
  11.9 11.3 %copy-start.34 = (s32[8]{0:T(128)S(1)}, s32[8]{0:T(128)}, u32[]{:S(2)}) copy-start(s32[8]{0:T(128)} %constant.217) | copy-start | bytes 100
  11.9 39.7 %copy-start.32 = (s32[1024]{0:T(1024)S(1)}, s32[1024]{0:T(1024)}, u32[]{:S(2)}) copy-start(s32[1024]{0:T(1024)} %param.18) | copy-start | bytes 12292
  12.1 53.4 %copy-start.3 = (bf16[512,1024]{1,0:T(8,128)(2,1)}, bf16[512,1024]{1,0:T(8,128)(2,1)S(1)}, u32[]{:S(2)}) copy-start(bf16[512,1024]{1,0:T(8,128)(2,1)S(1)} %pad_maximum_fusion.refs_8_) | copy-start | bytes 3145732
  12.1 37.8 %collective-permute-start.2 = (bf16[512,1024]{1,0:T(8,128)(2,1)S(1)}, bf16[512,1024]{1,0:T(8,128)(2,1)}, u32[]{:S(2)}, u32[]{:S(2)}) collective-permute-start(bf16[512,1024]{1,0:T(8,128)(2,1)S(1)} %pad_maximum_fusion.refs_8_), channel_id=1, source_target_pairs={{0,64},{1,65},{2,66},{3,67},{4,68},{5,69},{6,70},{7,71},{8,72},{9,... | collective-permute-start | bytes 3145736 | tf_op jit(solution)/shard_map/ppermute | solution.py:29
  13.4 36.5 %collective-permute-start.3 = (bf16[512,1024]{1,0:T(8,128)(2,1)S(1)}, bf16[512,1024]{1,0:T(8,128)(2,1)}, u32[]{:S(2)}, u32[]{:S(2)}) collective-permute-start(bf16[512,1024]{1,0:T(8,128)(2,1)S(1)} %pad_maximum_fusion.refs_8_), channel_id=1, source_target_pairs={{0,192},{1,193},{2,194},{3,195},{4,196},{5,197},{6,198},{7,199},{8... | collective-permute-start | bytes 3145736 | tf_op jit(solution)/shard_map/ppermute | solution.py:29
  14.9 35.1 %collective-permute-start.7 = (bf16[512,1024]{1,0:T(8,128)(2,1)S(1)}, bf16[512,1024]{1,0:T(8,128)(2,1)S(1)}, u32[]{:S(2)}, u32[]{:S(2)}) collective-permute-start(bf16[512,1024]{1,0:T(8,128)(2,1)S(1)} %pad_maximum_fusion.refs_8_), channel_id=1, source_target_pairs={{0,1},{1,0},{2,3},{3,2},{4,5},{5,4},{6,7},{7,6},{8,9},{9,8},{10,11... | collective-permute-start | bytes 3145736 | tf_op jit(solution)/shard_map/ppermute | solution.py:29
  16.1 16.1 %collective-permute-start = (bf16[112,1024]{1,0:T(8,128)(2,1)S(1)}, bf16[112,1024]{1,0:T(8,128)(2,1)S(1)}, u32[]{:S(2)}, u32[]{:S(2)}) collective-permute-start(bf16[112,1024]{1,0:T(8,128)(2,1)S(1)} %pad_maximum_fusion.2), channel_id=1, source_target_pairs={{0,0},{1,32},{2,2},{3,34},{4,4},{5,36},{6,6},{7,38},{8,64},{9,96},... | collective-permute-start | bytes 688136 | tf_op jit(solution)/shard_map/ppermute | solution.py:41
  32.2 33.3 %copy-start.18 = (bf16[112,1024]{1,0:T(8,128)(2,1)}, bf16[112,1024]{1,0:T(8,128)(2,1)S(1)}, u32[]{:S(2)}) copy-start(bf16[112,1024]{1,0:T(8,128)(2,1)S(1)} %collective-permute-done.refs_0_) | copy-start | bytes 688132
  32.2 5.3 %collective-permute-start.1 = (bf16[112,1024]{1,0:T(8,128)(2,1)S(1)}, bf16[112,1024]{1,0:T(8,128)(2,1)S(1)}, u32[]{:S(2)}, u32[]{:S(2)}) collective-permute-start(bf16[112,1024]{1,0:T(8,128)(2,1)S(1)} %collective-permute-done.refs_0_), channel_id=1, source_target_pairs={{0,8},{1,9},{2,10},{3,11},{4,12},{5,13},{6,14},{7,15},{8,16},{9,17... | collective-permute-start | bytes 688136 | tf_op jit(solution)/shard_map/ppermute | solution.py:29
  32.7 10.6 %collective-permute-start.5 = (bf16[112,1024]{1,0:T(8,128)(2,1)S(1)}, bf16[112,1024]{1,0:T(8,128)(2,1)S(1)}, u32[]{:S(2)}, u32[]{:S(2)}) collective-permute-start(bf16[112,1024]{1,0:T(8,128)(2,1)S(1)} %collective-permute-done.refs_0_), channel_id=1, source_target_pairs={{0,56},{1,57},{2,58},{3,59},{4,60},{5,61},{6,62},{7,63},{8,0},{9,1... | collective-permute-start | bytes 688136 | tf_op jit(solution)/shard_map/ppermute | solution.py:29
  37.4 28.0 %copy-start.19 = (bf16[112,1024]{1,0:T(8,128)(2,1)}, bf16[112,1024]{1,0:T(8,128)(2,1)S(1)}, u32[]{:S(2)}) copy-start(bf16[112,1024]{1,0:T(8,128)(2,1)S(1)} %collective-permute-done.1.refs_1_) | copy-start | bytes 688132
  37.4 8.4 %collective-permute-start.4 = (bf16[112,1024]{1,0:T(8,128)(2,1)S(1)}, bf16[112,1024]{1,0:T(8,128)(2,1)S(1)}, u32[]{:S(2)}, u32[]{:S(2)}) collective-permute-start(bf16[112,1024]{1,0:T(8,128)(2,1)S(1)} %collective-permute-done.1.refs_1_), channel_id=1, source_target_pairs={{0,8},{1,9},{2,10},{3,11},{4,12},{5,13},{6,14},{7,15},{8,16},{9,17... | collective-permute-start | bytes 688136 | tf_op jit(solution)/shard_map/ppermute | solution.py:29
  43.3 22.1 %copy-start.20 = (bf16[112,1024]{1,0:T(8,128)(2,1)}, bf16[112,1024]{1,0:T(8,128)(2,1)S(1)}, u32[]{:S(2)}) copy-start(bf16[112,1024]{1,0:T(8,128)(2,1)S(1)} %collective-permute-done.5.refs_5_) | copy-start | bytes 688132
  43.3 6.6 %collective-permute-start.6 = (bf16[112,1024]{1,0:T(8,128)(2,1)S(1)}, bf16[112,1024]{1,0:T(8,128)(2,1)S(1)}, u32[]{:S(2)}, u32[]{:S(2)}) collective-permute-start(bf16[112,1024]{1,0:T(8,128)(2,1)S(1)} %collective-permute-done.5.refs_5_), channel_id=1, source_target_pairs={{0,56},{1,57},{2,58},{3,59},{4,60},{5,61},{6,62},{7,63},{8,0},{9,1... | collective-permute-start | bytes 688136 | tf_op jit(solution)/shard_map/ppermute | solution.py:29
  45.9 19.6 %copy-start.21 = (bf16[112,1024]{1,0:T(8,128)(2,1)}, bf16[112,1024]{1,0:T(8,128)(2,1)S(1)}, u32[]{:S(2)}) copy-start(bf16[112,1024]{1,0:T(8,128)(2,1)S(1)} %collective-permute-done.4.refs_2_) | copy-start | bytes 688132
  49.9 15.6 %copy-start.22 = (bf16[112,1024]{1,0:T(8,128)(2,1)}, bf16[112,1024]{1,0:T(8,128)(2,1)S(1)}, u32[]{:S(2)}) copy-start(bf16[112,1024]{1,0:T(8,128)(2,1)S(1)} %collective-permute-done.6.refs_6_) | copy-start | bytes 688132
  50.0 15.5 %collective-permute-start.11 = (bf16[512,1024]{1,0:T(8,128)(2,1)}, bf16[512,1024]{1,0:T(8,128)(2,1)}, u32[]{:S(2)}, u32[]{:S(2)}) collective-permute-start(bf16[512,1024]{1,0:T(8,128)(2,1)} %collective-permute-done.2.refs_9_), channel_id=1, source_target_pairs={{0,1},{1,0},{2,3},{3,2},{4,5},{5,4},{6,7},{7,6},{8,9},{9,8},{10,11... | collective-permute-start | bytes 3145736 | tf_op jit(solution)/shard_map/ppermute | solution.py:29
  51.5 13.9 %collective-permute-start.12 = (bf16[512,1024]{1,0:T(8,128)(2,1)}, bf16[512,1024]{1,0:T(8,128)(2,1)}, u32[]{:S(2)}, u32[]{:S(2)}) collective-permute-start(bf16[512,1024]{1,0:T(8,128)(2,1)} %collective-permute-done.3.refs_10_), channel_id=1, source_target_pairs={{0,1},{1,0},{2,3},{3,2},{4,5},{5,4},{6,7},{7,6},{8,9},{9,8},{10,11... | collective-permute-start | bytes 3145736 | tf_op jit(solution)/shard_map/ppermute | solution.py:29
  52.2 25.8 %collective-permute-start.13 = (bf16[512,1024]{1,0:T(8,128)(2,1)}, bf16[512,1024]{1,0:T(8,128)(2,1)S(1)}, u32[]{:S(2)}, u32[]{:S(2)}) collective-permute-start(bf16[512,1024]{1,0:T(8,128)(2,1)} %collective-permute-done.2.refs_9_), channel_id=1, source_target_pairs={{0,64},{1,65},{2,66},{3,67},{4,68},{5,69},{6,70},{7,71},{8,72},{9,... | collective-permute-start | bytes 3145736 | tf_op jit(solution)/shard_map/ppermute | solution.py:29
  52.3 7.0 %collective-permute-start.8 = (bf16[112,1024]{1,0:T(8,128)(2,1)S(1)}, bf16[112,1024]{1,0:T(8,128)(2,1)}, u32[]{:S(2)}, u32[]{:S(2)}) collective-permute-start(bf16[112,1024]{1,0:T(8,128)(2,1)S(1)} %collective-permute-done.4.refs_2_), channel_id=1, source_target_pairs={{0,8},{1,9},{2,10},{3,11},{4,12},{5,13},{6,14},{7,15},{8,16},{9,17... | collective-permute-start | bytes 688136 | tf_op jit(solution)/shard_map/ppermute | solution.py:29
  54.6 7.8 %collective-permute-start.10 = (bf16[112,1024]{1,0:T(8,128)(2,1)S(1)}, bf16[112,1024]{1,0:T(8,128)(2,1)}, u32[]{:S(2)}, u32[]{:S(2)}) collective-permute-start(bf16[112,1024]{1,0:T(8,128)(2,1)S(1)} %collective-permute-done.6.refs_6_), channel_id=1, source_target_pairs={{0,56},{1,57},{2,58},{3,59},{4,60},{5,61},{6,62},{7,63},{8,0},{9,1... | collective-permute-start | bytes 688136 | tf_op jit(solution)/shard_map/ppermute | solution.py:29
  59.3 6.2 %collective-permute-start.9 = (bf16[112,1024]{1,0:T(8,128)(2,1)}, bf16[112,1024]{1,0:T(8,128)(2,1)}, u32[]{:S(2)}, u32[]{:S(2)}) collective-permute-start(bf16[112,1024]{1,0:T(8,128)(2,1)} %collective-permute-done.8.refs_3_), channel_id=1, source_target_pairs={{0,8},{1,9},{2,10},{3,11},{4,12},{5,13},{6,14},{7,15},{8,16},{9,17... | collective-permute-start | bytes 688136 | tf_op jit(solution)/shard_map/ppermute | solution.py:29
  78.0 8.4 %collective-permute-start.17 = (bf16[512,1024]{1,0:T(8,128)(2,1)S(1)}, bf16[512,1024]{1,0:T(8,128)(2,1)S(1)}, u32[]{:S(2)}, u32[]{:S(2)}) collective-permute-start(bf16[512,1024]{1,0:T(8,128)(2,1)S(1)} %collective-permute-done.13.refs_8_), channel_id=1, source_target_pairs={{0,1},{1,0},{2,3},{3,2},{4,5},{5,4},{6,7},{7,6},{8,9},{9,8},{10,11... | collective-permute-start | bytes 3145736 | tf_op jit(solution)/shard_map/ppermute | solution.py:29
  79.3 13.0 %copy-start.28 = (s32[4]{0:T(128)}, s32[4]{0:T(128)S(1)}, u32[]{:S(2)}) copy-start(s32[4]{0:T(128)S(1)} %get-tuple-element.76.xs) | copy-start | bytes 52
  79.6 13.4 %collective-permute-start.14 = (bf16[112,1536]{1,0:T(8,128)(2,1)}, bf16[112,1536]{1,0:T(8,128)(2,1)S(1)}, u32[]{:S(2)}, u32[]{:S(2)}) collective-permute-start(bf16[112,1536]{1,0:T(8,128)(2,1)} %get-tuple-element.55), channel_id=1, source_target_pairs={{0,4},{1,5},{2,6},{3,7},{4,0},{5,1},{6,2},{7,3},{8,12},{9,13},{10,... | collective-permute-start | bytes 1032200 | tf_op jit(solution)/shard_map/ppermute | solution.py:29
  82.6 16.4 %collective-permute-start.15 = (bf16[112,1536]{1,0:T(8,128)(2,1)}, bf16[112,1536]{1,0:T(8,128)(2,1)S(1)}, u32[]{:S(2)}, u32[]{:S(2)}) collective-permute-start(bf16[112,1536]{1,0:T(8,128)(2,1)} %get-tuple-element.56), channel_id=1, source_target_pairs={{0,2},{1,3},{2,4},{3,5},{4,6},{5,7},{6,0},{7,1},{8,10},{9,11},{10,... | collective-permute-start | bytes 1032200 | tf_op jit(solution)/shard_map/ppermute | solution.py:29
  83.1 15.9 %collective-permute-start.16 = (bf16[112,1536]{1,0:T(8,128)(2,1)}, bf16[112,1536]{1,0:T(8,128)(2,1)S(1)}, u32[]{:S(2)}, u32[]{:S(2)}) collective-permute-start(bf16[112,1536]{1,0:T(8,128)(2,1)} %get-tuple-element.57), channel_id=1, source_target_pairs={{0,6},{1,7},{2,0},{3,1},{4,2},{5,3},{6,4},{7,5},{8,14},{9,15},{10,... | collective-permute-start | bytes 1032200 | tf_op jit(solution)/shard_map/ppermute | solution.py:29
  92.3 8.6 %collective-permute-start.18 = (bf16[112,512]{1,0:T(8,128)(2,1)}, bf16[112,512]{1,0:T(8,128)(2,1)S(1)}, u32[]{:S(2)}, u32[]{:S(2)}) collective-permute-start(bf16[112,512]{1,0:T(8,128)(2,1)} %get-tuple-element.60), channel_id=1, source_target_pairs={{0,4},{1,5},{2,6},{3,7},{4,0},{5,1},{6,2},{7,3},{8,12},{9,13},{10,... | collective-permute-start | bytes 344072 | tf_op jit(solution)/shard_map/ppermute | solution.py:29
  92.4 11.2 %collective-permute-start.19 = (bf16[112,512]{1,0:T(8,128)(2,1)}, bf16[112,512]{1,0:T(8,128)(2,1)S(1)}, u32[]{:S(2)}, u32[]{:S(2)}) collective-permute-start(bf16[112,512]{1,0:T(8,128)(2,1)} %get-tuple-element.61), channel_id=1, source_target_pairs={{0,2},{1,3},{2,4},{3,5},{4,6},{5,7},{6,0},{7,1},{8,10},{9,11},{10,... | collective-permute-start | bytes 344072 | tf_op jit(solution)/shard_map/ppermute | solution.py:29
  93.0 10.8 %copy-start.15 = (bf16[112,1536]{1,0:T(8,128)(2,1)}, bf16[112,1536]{1,0:T(8,128)(2,1)S(1)}, u32[]{:S(2)}) copy-start(bf16[112,1536]{1,0:T(8,128)(2,1)S(1)} %collective-permute-done.14.refs_1_) | copy-start | bytes 1032196
  93.0 10.8 %collective-permute-start.20 = (bf16[112,512]{1,0:T(8,128)(2,1)}, bf16[112,512]{1,0:T(8,128)(2,1)S(1)}, u32[]{:S(2)}, u32[]{:S(2)}) collective-permute-start(bf16[112,512]{1,0:T(8,128)(2,1)} %get-tuple-element.62), channel_id=1, source_target_pairs={{0,6},{1,7},{2,0},{3,1},{4,2},{5,3},{6,4},{7,5},{8,14},{9,15},{10,... | collective-permute-start | bytes 344072 | tf_op jit(solution)/shard_map/ppermute | solution.py:29
  104.4 11.1 %copy-start.29 = (bf16[448]{0:T(512)(128)(2,1)S(1)}, bf16[448]{0:T(512)(128)(2,1)}, u32[]{:S(2)}) copy-start(bf16[448]{0:T(512)(128)(2,1)} %param.21) | copy-start | bytes 2692
  104.4 11.1 %copy-start.30 = (bf16[448]{0:T(512)(128)(2,1)S(1)}, bf16[448]{0:T(512)(128)(2,1)}, u32[]{:S(2)}) copy-start(bf16[448]{0:T(512)(128)(2,1)} %param.22) | copy-start | bytes 2692
  108.6 8.5 %copy-start.4 = (bf16[512,896]{1,0:T(8,128)(2,1)S(1)}, bf16[512,896]{1,0:T(8,128)(2,1)}, u32[]{:S(2)}) copy-start(bf16[512,896]{1,0:T(8,128)(2,1)} %param.23) | copy-start | bytes 2752516
  108.6 8.5 %copy-start.5 = (bf16[512,896]{1,0:T(8,128)(2,1)S(1)}, bf16[512,896]{1,0:T(8,128)(2,1)}, u32[]{:S(2)}) copy-start(bf16[512,896]{1,0:T(8,128)(2,1)} %param.24) | copy-start | bytes 2752516
  108.6 41.5 %all-to-all-start = ((bf16[32,112,128]{2,1,0:T(8,128)(2,1)}), bf16[32,112,128]{2,1,0:T(8,128)(2,1)S(1)}, u32[]{:S(2)}, u32[]{:S(2)}) async-start(bf16[32,112,128]{2,1,0:T(8,128)(2,1)} %send.1), calls=%async_computation | async-start | bytes 1835008 | tf_op jit(solution)/shard_map/all_to_all | solution.py:353
  127.9 52.7 %copy-start.31 = (s32[8]{0:T(128)S(1)}, s32[8]{0:T(128)}, u32[]{:S(2)}) copy-start(s32[8]{0:T(128)} %constant.211.clone) | copy-start | bytes 100
  154.4 11.6 %collective-permute-start.22 = (bf16[464,512]{1,0:T(8,128)(2,1)}, bf16[464,512]{1,0:T(8,128)(2,1)S(1)}, u32[]{:S(2)}, u32[]{:S(2)}) collective-permute-start(bf16[464,512]{1,0:T(8,128)(2,1)} %recv.1.refs_0_), channel_id=1, source_target_pairs={{0,2},{1,3},{2,4},{3,5},{4,6},{5,7},{6,0},{7,1},{8,10},{9,11},{10,... | collective-permute-start | bytes 1425416 | tf_op jit(solution)/shard_map/ppermute | solution.py:29
  155.6 14.8 %collective-permute-start.24 = (bf16[464,512]{1,0:T(8,128)(2,1)}, bf16[464,512]{1,0:T(8,128)(2,1)S(1)}, u32[]{:S(2)}, u32[]{:S(2)}) collective-permute-start(bf16[464,512]{1,0:T(8,128)(2,1)} %recv.1.refs_0_), channel_id=1, source_target_pairs={{0,6},{1,7},{2,0},{3,1},{4,2},{5,3},{6,4},{7,5},{8,14},{9,15},{10,... | collective-permute-start | bytes 1425416 | tf_op jit(solution)/shard_map/ppermute | solution.py:29
  157.1 21.6 %collective-permute-start.26 = (bf16[464,512]{1,0:T(8,128)(2,1)}, bf16[464,512]{1,0:T(8,128)(2,1)S(1)}, u32[]{:S(2)}, u32[]{:S(2)}) collective-permute-start(bf16[464,512]{1,0:T(8,128)(2,1)} %recv.1.refs_0_), channel_id=1, source_target_pairs={{0,4},{1,5},{2,6},{3,7},{4,0},{5,1},{6,2},{7,3},{8,12},{9,13},{10,... | collective-permute-start | bytes 1425416 | tf_op jit(solution)/shard_map/ppermute | solution.py:29
  158.3 22.9 %collective-permute-start.21 = (bf16[464,512]{1,0:T(8,128)(2,1)}, bf16[464,512]{1,0:T(8,128)(2,1)S(1)}, u32[]{:S(2)}, u32[]{:S(2)}) collective-permute-start(bf16[464,512]{1,0:T(8,128)(2,1)} %recv.1.refs_0_), channel_id=1, source_target_pairs={{0,1},{1,0},{2,3},{3,2},{4,5},{5,4},{6,7},{7,6},{8,9},{9,8},{10,11... | collective-permute-start | bytes 1425416 | tf_op jit(solution)/shard_map/ppermute | solution.py:29
  166.0 15.9 %copy-start.8 = (bf16[464,512]{1,0:T(8,128)(2,1)}, bf16[464,512]{1,0:T(8,128)(2,1)S(1)}, u32[]{:S(2)}) copy-start(bf16[464,512]{1,0:T(8,128)(2,1)S(1)} %collective-permute-done.22.refs_2_) | copy-start | bytes 1425412
  166.0 15.2 %collective-permute-start.23 = (bf16[464,512]{1,0:T(8,128)(2,1)S(1)}, bf16[464,512]{1,0:T(8,128)(2,1)S(1)}, u32[]{:S(2)}, u32[]{:S(2)}) collective-permute-start(bf16[464,512]{1,0:T(8,128)(2,1)S(1)} %collective-permute-done.22.refs_2_), channel_id=1, source_target_pairs={{0,1},{1,0},{2,3},{3,2},{4,5},{5,4},{6,7},{7,6},{8,9},{9,8},{10,11... | collective-permute-start | bytes 1425416 | tf_op jit(solution)/shard_map/ppermute | solution.py:29
  170.4 11.6 %copy-start.9 = (bf16[464,512]{1,0:T(8,128)(2,1)}, bf16[464,512]{1,0:T(8,128)(2,1)S(1)}, u32[]{:S(2)}) copy-start(bf16[464,512]{1,0:T(8,128)(2,1)S(1)} %collective-permute-done.24.refs_4_) | copy-start | bytes 1425412
  170.4 10.9 %collective-permute-start.25 = (bf16[464,512]{1,0:T(8,128)(2,1)S(1)}, bf16[464,512]{1,0:T(8,128)(2,1)S(1)}, u32[]{:S(2)}, u32[]{:S(2)}) collective-permute-start(bf16[464,512]{1,0:T(8,128)(2,1)S(1)} %collective-permute-done.24.refs_4_), channel_id=1, source_target_pairs={{0,1},{1,0},{2,3},{3,2},{4,5},{5,4},{6,7},{7,6},{8,9},{9,8},{10,11... | collective-permute-start | bytes 1425416 | tf_op jit(solution)/shard_map/ppermute | solution.py:29
  178.7 3.2 %collective-permute-start.27 = (bf16[464,512]{1,0:T(8,128)(2,1)S(1)}, bf16[464,512]{1,0:T(8,128)(2,1)S(1)}, u32[]{:S(2)}, u32[]{:S(2)}) collective-permute-start(bf16[464,512]{1,0:T(8,128)(2,1)S(1)} %collective-permute-done.26.refs_6_), channel_id=1, source_target_pairs={{0,1},{1,0},{2,3},{3,2},{4,5},{5,4},{6,7},{7,6},{8,9},{9,8},{10,11... | collective-permute-start | bytes 1425416 | tf_op jit(solution)/shard_map/ppermute | solution.py:29
  (18 other events, 44.0 us)
Sparse Core Ops, SparseCore 0:
  11.0 51.4 all-gather.2
  65.1 102.6 all-gather.4
where the time goes:
time: 206 us; the launch traced here: 205 us
  waiting for transfers between devices  71.1 us (35%)
  starting transfers between devices  58.5 us (28%)
  Pallas kernels  42.8 us (21%)
  between operations  14.6 us (7%)
  other arithmetic  9.24 us (4%)
  local copies, waits for them, and re-layouts  9.01 us (4%)
    ppermute x27, starting transfers between devices, move(): return lax.ppermute(value, AXES, pairs)  44.5 us
    ppermute x27, waiting for transfers between devices, move(): return lax.ppermute(value, AXES, pairs)  39.9 us
    all_to_all x1, waiting for transfers between devices, per_device(): arrived = lax.all_to_all(outgoing, 'dp', 0, 0, tiled=True)  22.2 us
    pallas_call x1, Pallas kernels, per_device(): call(final_kernel, (jax.ShapeDtypeStruct((448, 512), BF), jax.ShapeDtypeS...  15.2 us
    pallas_call x2, Pallas kernels, part(): call(part_kernel, (jax.ShapeDtypeStruct((112, size), BF),) * 4, 2, 8 + 2...  12.4 us
    ppermute x1, waiting for transfers between devices, spread_columns(): return lax.ppermute(shard, AXES, pairs)  8.97 us
    pallas_call x1, Pallas kernels, per_device(): call(stats_kernel, jax.ShapeDtypeStruct((8, 512), F32), 0, 1, 3584 * 512...  7.64 us
    ppermute x1, starting transfers between devices, spread_columns(): return lax.ppermute(shard, AXES, pairs)  7.06 us
  transfers between devices with their start and end apart: 31, of which 16 were waited for; matrix products, arithmetic and copies ran while one was open for 5% of the time, Pallas kernels for 10%

commit v1 on v0

--- a/solution.py
+++ b/solution.py
@@ -187,7 +187,7 @@
 
 def final_kernel(heads, *refs):
     grads, (weight, bundle, slope, active, stats, resid_grad, gate, up) = refs[:8], refs[8:16]
-    grad_buf, weight_buf, held, scale_buf, stat_buf, value, sems = refs[16:]
+    grad_buf, weight_buf, held, scale_buf, stat_buf, value, even, odd, sems = refs[16:]
     copies = [pltpu.make_async_copy(stats, stat_buf, sems.at[26])]
     for k in range(8):
         copies.append(pltpu.make_async_copy(grads[k], grad_buf.at[k], sems.at[k]))
@@ -205,25 +205,38 @@
     for copy in copies[:9]:
         copy.wait()
     out_scale, resid_scale, pull, push = row_factors(stat_buf, grad_buf)
-    value[...] = jnp.zeros((512, 896), F32)
-
-    @pl.loop(0, 8)
-    def _(k):
+
+    def arrive(k):
         pltpu.make_async_copy(bundle.at[pl.ds(0, 912)], held.at[k], sems.at[8 + k]).wait()
         pltpu.make_async_copy(weight.at[pl.ds(0, 448)], weight_buf.at[k], sems.at[16 + k]).wait()
+
+    def totals(k):
         gains = held[k, 896:912, :].astype(F32).T
         gain_post, gain_final = gains[:448, 0:1], gains[:448, 1:2]
         out = held[k, 448:896, :].astype(F32)
         resid = held[k, 0:448, :].astype(F32) + out * gain_post * out_scale
         norm_grad = grad_buf[k, 0:448, :].astype(F32) * gain_final
         total = resid_scale * (norm_grad - resid * pull)
-
-        @pl.when(k == 0)
+        return total, (out_scale * (total * gain_post - out * push)).astype(BF)
+
+    arrive(0)
+    total, post = totals(0)
+    resid_grad[...] = total.astype(BF)
+    even[...] = post
+    value[...] = jnp.zeros((512, 896), F32)
+
+    @pl.loop(0, 4)
+    def _(pair):
+        arrive(2 * pair + 1)
+        odd[...] = totals(2 * pair + 1)[1]
+        value[...] += dot_tn(even[...], weight_buf[2 * pair])
+
+        @pl.when(pair < 3)
         def _():
-            resid_grad[...] = total.astype(BF)
-
-        post = out_scale * (total * gain_post - out * push)
-        value[...] += dot_tn(post.astype(BF), weight_buf[k])
+            arrive(2 * pair + 2)
+
+        even[...] = totals(jnp.minimum(2 * pair + 2, 7))[1]
+        value[...] += dot_tn(odd[...], weight_buf[2 * pair + 1])
 
     for copy in copies[25:]:
         copy.wait()
@@ -394,6 +407,8 @@
             pltpu.VMEM((2, 512, 896), F32),
             pltpu.VMEM((8, 512), F32),
             pltpu.VMEM((512, 896), F32),
+            pltpu.VMEM((448, 512), BF),
+            pltpu.VMEM((448, 512), BF),
             pltpu.SemaphoreType.DMA((27,)),
         ],
         name="final",

time: 206 us -> 204 us (level)
  no operation moved by 1% of the time
where the time goes in v1:
time: 204 us; the launch traced here: 203 us
  waiting for transfers between devices  71.1 us (35%)
  starting transfers between devices  58.5 us (29%)
  Pallas kernels  41.1 us (20%)
  between operations  14.6 us (7%)
  other arithmetic  9.24 us (5%)
  local copies, waits for them, and re-layouts  9.01 us (4%)
    ppermute x27, starting transfers between devices, move(): return lax.ppermute(value, AXES, pairs)  44.5 us
    ppermute x27, waiting for transfers between devices, move(): return lax.ppermute(value, AXES, pairs)  39.9 us
    all_to_all x1, waiting for transfers between devices, per_device(): arrived = lax.all_to_all(outgoing, 'dp', 0, 0, tiled=True)  22.2 us
    pallas_call x1, Pallas kernels, per_device(): call(final_kernel, (jax.ShapeDtypeStruct((448, 512), BF), jax.ShapeDtypeS...  13.5 us
    pallas_call x2, Pallas kernels, part(): call(part_kernel, (jax.ShapeDtypeStruct((112, size), BF),) * 4, 2, 8 + 2...  12.4 us
    ppermute x1, waiting for transfers between devices, spread_columns(): return lax.ppermute(shard, AXES, pairs)  8.97 us
    pallas_call x1, Pallas kernels, per_device(): call(stats_kernel, jax.ShapeDtypeStruct((8, 512), F32), 0, 1, 3584 * 512...  7.64 us
    ppermute x1, starting transfers between devices, spread_columns(): return lax.ppermute(shard, AXES, pairs)  7.06 us
  transfers between devices with their start and end apart: 31, of which 16 were waited for; matrix products, arithmetic and copies ran while one was open for 5% of the time, Pallas kernels for 10%

profile of v1, /device:TPU:33, one launch (start us, length us, event | category | flops | bytes accessed | tf_op | source)
XLA Modules:
  0.0 203.4 jit_solution(16003410114396809735)
XLA Ops:
  8.7 2.2 %pad_maximum_fusion.1 = bf16[912,512]{1,0:T(8,128)(2,1)} fusion(bf16[16,512]{1,0:T(8,128)(2,1)S(1)} %fusion.14, bf16[448,512]{1,0:T(8,128)(2,1)} %bitcast.33, bf16[448,512]{1,0:T(8,128)(2,1)} %bitcast.31), kind=kLoop, calls=%fused_computation.16 | loop fusion | flops 2801664 | bytes 1867776 | tf_op jit(solution)/shard_map/concatenate | solution.py:308
  11.1 0.8 copy-done.7
  12.1 1.3 collective-permute-start.2
  13.4 1.5 collective-permute-start.3
  14.9 1.2 collective-permute-start.7
  16.1 7.1 %collective-permute-start = (bf16[112,1024]{1,0:T(8,128)(2,1)S(1)}, bf16[112,1024]{1,0:T(8,128)(2,1)S(1)}, u32[]{:S(2)}, u32[]{:S(2)}) collective-permute-start(bf16[112,1024]{1,0:T(8,128)(2,1)S(1)} %pad_maximum_fusion.2), channel_id=1, source_target_pairs={{0,0},{1,32},{2,2},{3,34},{4,4},{5,36},{6,6},{7,38},{8,64},{9,96},... | collective-permute-start | bytes 688136 | tf_op jit(solution)/shard_map/ppermute | solution.py:41
  23.2 9.0 %collective-permute-done.refs_0_ = bf16[112,1024]{1,0:T(8,128)(2,1)S(1)} collective-permute-done((bf16[112,1024]{1,0:T(8,128)(2,1)S(1)}, bf16[112,1024]{1,0:T(8,128)(2,1)S(1)}, u32[]{:S(2)}, u32[]{:S(2)}) %collective-permute-start) | collective-permute-done | bytes 229408 | tf_op jit(solution)/shard_map/ppermute | solution.py:41
  32.7 0.9 collective-permute-start.5
  33.6 3.8 %collective-permute-done.1.refs_1_ = bf16[112,1024]{1,0:T(8,128)(2,1)S(1)} collective-permute-done((bf16[112,1024]{1,0:T(8,128)(2,1)S(1)}, bf16[112,1024]{1,0:T(8,128)(2,1)S(1)}, u32[]{:S(2)}, u32[]{:S(2)}) %collective-permute-start.1) | collective-permute-done | bytes 229408 | tf_op jit(solution)/shard_map/ppermute | solution.py:29
  37.4 3.9 %collective-permute-start.4 = (bf16[112,1024]{1,0:T(8,128)(2,1)S(1)}, bf16[112,1024]{1,0:T(8,128)(2,1)S(1)}, u32[]{:S(2)}, u32[]{:S(2)}) collective-permute-start(bf16[112,1024]{1,0:T(8,128)(2,1)S(1)} %collective-permute-done.1.refs_1_), channel_id=1, source_target_pairs={{0,8},{1,9},{2,10},{3,11},{4,12},{5,13},{6,14},{7,15},{8,16},{9,17... | collective-permute-start | bytes 688136 | tf_op jit(solution)/shard_map/ppermute | solution.py:29
  41.3 2.0 collective-permute-done.5.refs_5_
  43.3 2.5 %collective-permute-done.4.refs_2_ = bf16[112,1024]{1,0:T(8,128)(2,1)S(1)} collective-permute-done((bf16[112,1024]{1,0:T(8,128)(2,1)S(1)}, bf16[112,1024]{1,0:T(8,128)(2,1)S(1)}, u32[]{:S(2)}, u32[]{:S(2)}) %collective-permute-start.4) | collective-permute-done | bytes 229408 | tf_op jit(solution)/shard_map/ppermute | solution.py:29
  45.9 4.0 %collective-permute-done.6.refs_6_ = bf16[112,1024]{1,0:T(8,128)(2,1)S(1)} collective-permute-done((bf16[112,1024]{1,0:T(8,128)(2,1)S(1)}, bf16[112,1024]{1,0:T(8,128)(2,1)S(1)}, u32[]{:S(2)}, u32[]{:S(2)}) %collective-permute-start.6) | collective-permute-done | bytes 229408 | tf_op jit(solution)/shard_map/ppermute | solution.py:29
  50.0 1.5 collective-permute-start.11
  52.3 1.5 collective-permute-start.8
  54.7 4.5 %collective-permute-done.8.refs_3_ = bf16[112,1024]{1,0:T(8,128)(2,1)} collective-permute-done((bf16[112,1024]{1,0:T(8,128)(2,1)S(1)}, bf16[112,1024]{1,0:T(8,128)(2,1)}, u32[]{:S(2)}, u32[]{:S(2)}) %collective-permute-start.8) | collective-permute-done | bytes 229408 | tf_op jit(solution)/shard_map/ppermute | solution.py:29
  59.3 1.4 collective-permute-start.9
  61.5 0.9 collective-permute-done.10.refs_7_
  62.4 3.0 %collective-permute-done.9.refs_4_ = bf16[112,1024]{1,0:T(8,128)(2,1)} collective-permute-done((bf16[112,1024]{1,0:T(8,128)(2,1)}, bf16[112,1024]{1,0:T(8,128)(2,1)}, u32[]{:S(2)}, u32[]{:S(2)}) %collective-permute-start.9) | collective-permute-done | bytes 229408 | tf_op jit(solution)/shard_map/ppermute | solution.py:29
  65.5 7.5 %part.2 = (bf16[112,1536]{1,0:T(8,128)(2,1)}, bf16[112,1536]{1,0:T(8,128)(2,1)}, bf16[112,1536]{1,0:T(8,128)(2,1)}, bf16[112,1536]{1,0:T(8,128)(2,1)}) custom-call(s32[8]{0:T(128)} %fusion.25.where, s32[1]{0:T(128)} %bitcast.12.core, bf16[112,1024]{1,0:T(8,128)(2,1)} %copy-done.18, bf16[112,1024]{1,0:T(8,128)(2,1)} %copy-done.19, ...), custom_call_target="tpu_custom_call" | custom-call | flops 2818572288 | bytes 6000000 | tf_op jit(solution)/shard_map/part/pallas_call | solution.py:333
  73.0 5.0 %collective-permute-done.13.refs_8_ = bf16[512,1024]{1,0:T(8,128)(2,1)S(1)} collective-permute-done((bf16[512,1024]{1,0:T(8,128)(2,1)}, bf16[512,1024]{1,0:T(8,128)(2,1)S(1)}, u32[]{:S(2)}, u32[]{:S(2)}) %collective-permute-start.13) | collective-permute-done | bytes 1048608 | tf_op jit(solution)/shard_map/ppermute | solution.py:29
  78.0 1.2 collective-permute-start.17
  79.6 2.9 %collective-permute-start.14 = (bf16[112,1536]{1,0:T(8,128)(2,1)}, bf16[112,1536]{1,0:T(8,128)(2,1)S(1)}, u32[]{:S(2)}, u32[]{:S(2)}) collective-permute-start(bf16[112,1536]{1,0:T(8,128)(2,1)} %get-tuple-element.55), channel_id=1, source_target_pairs={{0,4},{1,5},{2,6},{3,7},{4,0},{5,1},{6,2},{7,3},{8,12},{9,13},{10,... | collective-permute-start | bytes 1032200 | tf_op jit(solution)/shard_map/ppermute | solution.py:29
  83.1 2.3 %collective-permute-start.16 = (bf16[112,1536]{1,0:T(8,128)(2,1)}, bf16[112,1536]{1,0:T(8,128)(2,1)S(1)}, u32[]{:S(2)}, u32[]{:S(2)}) collective-permute-start(bf16[112,1536]{1,0:T(8,128)(2,1)} %get-tuple-element.57), channel_id=1, source_target_pairs={{0,6},{1,7},{2,0},{3,1},{4,2},{5,3},{6,4},{7,5},{8,14},{9,15},{10,... | collective-permute-start | bytes 1032200 | tf_op jit(solution)/shard_map/ppermute | solution.py:29
  86.4 1.0 copy-done.2
  87.4 4.9 %part.3 = (bf16[112,512]{1,0:T(8,128)(2,1)}, bf16[112,512]{1,0:T(8,128)(2,1)}, bf16[112,512]{1,0:T(8,128)(2,1)}, bf16[112,512]{1,0:T(8,128)(2,1)}) custom-call(s32[8]{0:T(128)} %fusion.25.where, s32[1]{0:T(128)} %bitcast.12.core, bf16[112,1024]{1,0:T(8,128)(2,1)} %copy-done.18, bf16[112,1024]{1,0:T(8,128)(2,1)} %copy-done.19, bf16[112,1024]{1,0:T(8,128)(2,1)} %copy-done.21, ...), custom_call_target="tpu_custom_call" | custom-call | flops 939524096 | bytes 6000000 | tf_op jit(solution)/shard_map/part/pallas_call | solution.py:333
  93.0 2.2 %collective-permute-start.20 = (bf16[112,512]{1,0:T(8,128)(2,1)}, bf16[112,512]{1,0:T(8,128)(2,1)S(1)}, u32[]{:S(2)}, u32[]{:S(2)}) collective-permute-start(bf16[112,512]{1,0:T(8,128)(2,1)} %get-tuple-element.62), channel_id=1, source_target_pairs={{0,6},{1,7},{2,0},{3,1},{4,2},{5,3},{6,4},{7,5},{8,14},{9,15},{10,... | collective-permute-start | bytes 344072 | tf_op jit(solution)/shard_map/ppermute | solution.py:29
  95.8 3.2 %collective-permute-done.15.refs_2_ = bf16[112,1536]{1,0:T(8,128)(2,1)S(1)} collective-permute-done((bf16[112,1536]{1,0:T(8,128)(2,1)}, bf16[112,1536]{1,0:T(8,128)(2,1)S(1)}, u32[]{:S(2)}, u32[]{:S(2)}) %collective-permute-start.15) | collective-permute-done | bytes 344096 | tf_op jit(solution)/shard_map/ppermute | solution.py:29
  99.0 1.9 collective-permute-done.18.refs_5_
  100.9 2.7 %collective-permute-done.19.refs_6_ = bf16[112,512]{1,0:T(8,128)(2,1)S(1)} collective-permute-done((bf16[112,512]{1,0:T(8,128)(2,1)}, bf16[112,512]{1,0:T(8,128)(2,1)S(1)}, u32[]{:S(2)}, u32[]{:S(2)}) %collective-permute-start.19) | collective-permute-done | bytes 114720 | tf_op jit(solution)/shard_map/ppermute | solution.py:29
  104.4 4.3 %send.1 = bf16[32,112,128]{2,1,0:T(8,128)(2,1)} custom-call(s32[4]{0:T(128)} %copy-done.28, bf16[112,1536]{1,0:T(8,128)(2,1)} %get-tuple-element.54.refs_0_, bf16[112,1536]{1,0:T(8,128)(2,1)} %copy-done.15, bf16[112,1536]{1,0:T(8,128)(2,1)} %copy-done.16, bf16[112,1536]{1,0:T(8,128)(2,1)} %copy-done.17, bf16[112,512]{1,0:T(8,128)(2,1)} %get-tuple-element.59.refs_4_, ...), custom_call_target="tpu_custom_call" | custom-call | flops 469762048 | bytes 6000000 | tf_op jit(solution)/shard_map/send/pallas_call | solution.py:357
  108.6 6.8 %all-to-all-start = ((bf16[32,112,128]{2,1,0:T(8,128)(2,1)}), bf16[32,112,128]{2,1,0:T(8,128)(2,1)S(1)}, u32[]{:S(2)}, u32[]{:S(2)}) async-start(bf16[32,112,128]{2,1,0:T(8,128)(2,1)} %send.1), calls=%async_computation | async-start | bytes 1835008 | tf_op jit(solution)/shard_map/all_to_all | solution.py:366
  115.5 0.8 copy.19.gain_post
  116.3 0.8 copy.20.gain_final
  117.2 3.1 %fusion.3 = (f32[512,896]{1,0:T(8,128)}, f32[512,896]{1,0:T(8,128)}) fusion(bf16[512,896]{1,0:T(8,128)(2,1)S(1)} %copy-done.4, bf16[512,896]{1,0:T(8,128)(2,1)S(1)} %copy-done.5), kind=kLoop, calls=%fused_computation.10 | loop fusion | flops 9633792 | bytes 5505024 | tf_op jit(solution)/shard_map/mul | solution.py:323
  120.3 7.6 %stats.1.refs_12_ = f32[8,512]{1,0:T(8,128)} custom-call(bf16[7296,512]{1,0:T(8,128)(2,1)} %all-gather.3.cloned.1.call-done.bundle.refs_9_), custom_call_target="tpu_custom_call" | custom-call | flops 22020096 | bytes 6000000 | tf_op jit(solution)/shard_map/stats/pallas_call | solution.py:367
  127.9 22.2 %all-to-all-done.arrived = bf16[32,112,128]{2,1,0:T(8,128)(2,1)S(1)} async-done(((bf16[32,112,128]{2,1,0:T(8,128)(2,1)}), bf16[32,112,128]{2,1,0:T(8,128)(2,1)S(1)}, u32[]{:S(2)}, u32[]{:S(2)}) %all-to-all-start) | async-done | bytes 917536 | tf_op jit(solution)/shard_map/all_to_all | solution.py:366
  150.2 0.9 copy-done
  151.1 3.3 %recv.1.refs_0_ = bf16[464,512]{1,0:T(8,128)(2,1)} custom-call(bf16[32,112,128]{2,1,0:T(8,128)(2,1)} %copy-done, s32[1,512]{1,0:T(1,128)} %add.273.row_pos, bf16[448,512]{1,0:T(8,128)(2,1)} %bitcast.32, bf16[448,512]{1,0:T(8,128)(2,1)} %bitcast.34, f32[448,1]{1,0:T(8,128)} %copy.19.gain_post, f32[448,1]{1,0:T(8,128)} %copy.20.gain_final, f32[8,512]{1,0:T(8,128)} %stats.1.refs_12_), custom_call_target="tpu_custom_call" | custom-call | flops 469762048 | bytes 6000000 | tf_op jit(solution)/shard_map/recv/pallas_call | solution.py:379
  154.4 1.2 collective-permute-start.22
  155.6 1.5 collective-permute-start.24
  157.1 1.2 collective-permute-start.26
  158.3 2.4 %collective-permute-start.21 = (bf16[464,512]{1,0:T(8,128)(2,1)}, bf16[464,512]{1,0:T(8,128)(2,1)S(1)}, u32[]{:S(2)}, u32[]{:S(2)}) collective-permute-start(bf16[464,512]{1,0:T(8,128)(2,1)} %recv.1.refs_0_), channel_id=1, source_target_pairs={{0,1},{1,0},{2,3},{3,2},{4,5},{5,4},{6,7},{7,6},{8,9},{9,8},{10,11... | collective-permute-start | bytes 1425416 | tf_op jit(solution)/shard_map/ppermute | solution.py:29
  160.7 5.3 %collective-permute-done.22.refs_2_ = bf16[464,512]{1,0:T(8,128)(2,1)S(1)} collective-permute-done((bf16[464,512]{1,0:T(8,128)(2,1)}, bf16[464,512]{1,0:T(8,128)(2,1)S(1)}, u32[]{:S(2)}, u32[]{:S(2)}) %collective-permute-start.22) | collective-permute-done | bytes 475168 | tf_op jit(solution)/shard_map/ppermute | solution.py:29
  166.0 4.3 %collective-permute-start.23 = (bf16[464,512]{1,0:T(8,128)(2,1)S(1)}, bf16[464,512]{1,0:T(8,128)(2,1)S(1)}, u32[]{:S(2)}, u32[]{:S(2)}) collective-permute-start(bf16[464,512]{1,0:T(8,128)(2,1)S(1)} %collective-permute-done.22.refs_2_), channel_id=1, source_target_pairs={{0,1},{1,0},{2,3},{3,2},{4,5},{5,4},{6,7},{7,6},{8,9},{9,8},{10,11... | collective-permute-start | bytes 1425416 | tf_op jit(solution)/shard_map/ppermute | solution.py:29
  170.4 8.4 %collective-permute-start.25 = (bf16[464,512]{1,0:T(8,128)(2,1)S(1)}, bf16[464,512]{1,0:T(8,128)(2,1)S(1)}, u32[]{:S(2)}, u32[]{:S(2)}) collective-permute-start(bf16[464,512]{1,0:T(8,128)(2,1)S(1)} %collective-permute-done.24.refs_4_), channel_id=1, source_target_pairs={{0,1},{1,0},{2,3},{3,2},{4,5},{5,4},{6,7},{7,6},{8,9},{9,8},{10,11... | collective-permute-start | bytes 1425416 | tf_op jit(solution)/shard_map/ppermute | solution.py:29
  178.7 1.8 collective-permute-start.27
  183.1 13.5 %final.1 = (bf16[448,512]{1,0:T(8,128)(2,1)}, bf16[512,896]{1,0:T(8,128)(2,1)}, bf16[512,896]{1,0:T(8,128)(2,1)}) custom-call(s32[8]{0:T(128)} %fusion.24.heads, bf16[464,512]{1,0:T(8,128)(2,1)} %recv.1.refs_0_, bf16[464,512]{1,0:T(8,128)(2,1)} %copy-done.11, bf16[464,512]{1,0:T(8,128)(2,1)} %copy-done.8, bf16[464,512]{1,0:T(8,128)(2,1)} %copy-done.12, ...), custom_call_target="tpu_custom_call" | custom-call | flops 3288334336 | bytes 6000000 | tf_op jit(solution)/shard_map/final/pallas_call | solution.py:393
  (130 shorter events, 11.4 us)
Async XLA Ops:
  7.2 113.1 %all-gather.3.cloned.1.call-start = ((), (), s32[]{:S(2)}) async-start(), calls=%async_computation.1 | async-start | bytes 8404992 | tf_op jit(solution)/shard_map/all_gather | solution.py:309
  10.9 170.3 %all-gather.5.cloned.1.call-start = ((), (), s32[]{:S(2)}) async-start(), calls=%async_computation.2 | async-start | bytes 6623232 | tf_op jit(solution)/shard_map/all_gather | solution.py:325
  11.9 11.3 %copy-start.34 = (s32[8]{0:T(128)S(1)}, s32[8]{0:T(128)}, u32[]{:S(2)}) copy-start(s32[8]{0:T(128)} %constant.217) | copy-start | bytes 100
  11.9 39.7 %copy-start.32 = (s32[1024]{0:T(1024)S(1)}, s32[1024]{0:T(1024)}, u32[]{:S(2)}) copy-start(s32[1024]{0:T(1024)} %param.18) | copy-start | bytes 12292
  12.1 53.4 %copy-start.3 = (bf16[512,1024]{1,0:T(8,128)(2,1)}, bf16[512,1024]{1,0:T(8,128)(2,1)S(1)}, u32[]{:S(2)}) copy-start(bf16[512,1024]{1,0:T(8,128)(2,1)S(1)} %pad_maximum_fusion.refs_8_) | copy-start | bytes 3145732
  12.1 37.8 %collective-permute-start.2 = (bf16[512,1024]{1,0:T(8,128)(2,1)S(1)}, bf16[512,1024]{1,0:T(8,128)(2,1)}, u32[]{:S(2)}, u32[]{:S(2)}) collective-permute-start(bf16[512,1024]{1,0:T(8,128)(2,1)S(1)} %pad_maximum_fusion.refs_8_), channel_id=1, source_target_pairs={{0,64},{1,65},{2,66},{3,67},{4,68},{5,69},{6,70},{7,71},{8,72},{9,... | collective-permute-start | bytes 3145736 | tf_op jit(solution)/shard_map/ppermute | solution.py:29
  13.4 36.5 %collective-permute-start.3 = (bf16[512,1024]{1,0:T(8,128)(2,1)S(1)}, bf16[512,1024]{1,0:T(8,128)(2,1)}, u32[]{:S(2)}, u32[]{:S(2)}) collective-permute-start(bf16[512,1024]{1,0:T(8,128)(2,1)S(1)} %pad_maximum_fusion.refs_8_), channel_id=1, source_target_pairs={{0,192},{1,193},{2,194},{3,195},{4,196},{5,197},{6,198},{7,199},{8... | collective-permute-start | bytes 3145736 | tf_op jit(solution)/shard_map/ppermute | solution.py:29
  14.9 35.1 %collective-permute-start.7 = (bf16[512,1024]{1,0:T(8,128)(2,1)S(1)}, bf16[512,1024]{1,0:T(8,128)(2,1)S(1)}, u32[]{:S(2)}, u32[]{:S(2)}) collective-permute-start(bf16[512,1024]{1,0:T(8,128)(2,1)S(1)} %pad_maximum_fusion.refs_8_), channel_id=1, source_target_pairs={{0,1},{1,0},{2,3},{3,2},{4,5},{5,4},{6,7},{7,6},{8,9},{9,8},{10,11... | collective-permute-start | bytes 3145736 | tf_op jit(solution)/shard_map/ppermute | solution.py:29
  16.1 16.1 %collective-permute-start = (bf16[112,1024]{1,0:T(8,128)(2,1)S(1)}, bf16[112,1024]{1,0:T(8,128)(2,1)S(1)}, u32[]{:S(2)}, u32[]{:S(2)}) collective-permute-start(bf16[112,1024]{1,0:T(8,128)(2,1)S(1)} %pad_maximum_fusion.2), channel_id=1, source_target_pairs={{0,0},{1,32},{2,2},{3,34},{4,4},{5,36},{6,6},{7,38},{8,64},{9,96},... | collective-permute-start | bytes 688136 | tf_op jit(solution)/shard_map/ppermute | solution.py:41
  32.2 33.3 %copy-start.18 = (bf16[112,1024]{1,0:T(8,128)(2,1)}, bf16[112,1024]{1,0:T(8,128)(2,1)S(1)}, u32[]{:S(2)}) copy-start(bf16[112,1024]{1,0:T(8,128)(2,1)S(1)} %collective-permute-done.refs_0_) | copy-start | bytes 688132
  32.2 5.3 %collective-permute-start.1 = (bf16[112,1024]{1,0:T(8,128)(2,1)S(1)}, bf16[112,1024]{1,0:T(8,128)(2,1)S(1)}, u32[]{:S(2)}, u32[]{:S(2)}) collective-permute-start(bf16[112,1024]{1,0:T(8,128)(2,1)S(1)} %collective-permute-done.refs_0_), channel_id=1, source_target_pairs={{0,8},{1,9},{2,10},{3,11},{4,12},{5,13},{6,14},{7,15},{8,16},{9,17... | collective-permute-start | bytes 688136 | tf_op jit(solution)/shard_map/ppermute | solution.py:29
  32.7 10.6 %collective-permute-start.5 = (bf16[112,1024]{1,0:T(8,128)(2,1)S(1)}, bf16[112,1024]{1,0:T(8,128)(2,1)S(1)}, u32[]{:S(2)}, u32[]{:S(2)}) collective-permute-start(bf16[112,1024]{1,0:T(8,128)(2,1)S(1)} %collective-permute-done.refs_0_), channel_id=1, source_target_pairs={{0,56},{1,57},{2,58},{3,59},{4,60},{5,61},{6,62},{7,63},{8,0},{9,1... | collective-permute-start | bytes 688136 | tf_op jit(solution)/shard_map/ppermute | solution.py:29
  37.4 28.0 %copy-start.19 = (bf16[112,1024]{1,0:T(8,128)(2,1)}, bf16[112,1024]{1,0:T(8,128)(2,1)S(1)}, u32[]{:S(2)}) copy-start(bf16[112,1024]{1,0:T(8,128)(2,1)S(1)} %collective-permute-done.1.refs_1_) | copy-start | bytes 688132
  37.4 8.4 %collective-permute-start.4 = (bf16[112,1024]{1,0:T(8,128)(2,1)S(1)}, bf16[112,1024]{1,0:T(8,128)(2,1)S(1)}, u32[]{:S(2)}, u32[]{:S(2)}) collective-permute-start(bf16[112,1024]{1,0:T(8,128)(2,1)S(1)} %collective-permute-done.1.refs_1_), channel_id=1, source_target_pairs={{0,8},{1,9},{2,10},{3,11},{4,12},{5,13},{6,14},{7,15},{8,16},{9,17... | collective-permute-start | bytes 688136 | tf_op jit(solution)/shard_map/ppermute | solution.py:29
  43.3 22.1 %copy-start.20 = (bf16[112,1024]{1,0:T(8,128)(2,1)}, bf16[112,1024]{1,0:T(8,128)(2,1)S(1)}, u32[]{:S(2)}) copy-start(bf16[112,1024]{1,0:T(8,128)(2,1)S(1)} %collective-permute-done.5.refs_5_) | copy-start | bytes 688132
  43.3 6.6 %collective-permute-start.6 = (bf16[112,1024]{1,0:T(8,128)(2,1)S(1)}, bf16[112,1024]{1,0:T(8,128)(2,1)S(1)}, u32[]{:S(2)}, u32[]{:S(2)}) collective-permute-start(bf16[112,1024]{1,0:T(8,128)(2,1)S(1)} %collective-permute-done.5.refs_5_), channel_id=1, source_target_pairs={{0,56},{1,57},{2,58},{3,59},{4,60},{5,61},{6,62},{7,63},{8,0},{9,1... | collective-permute-start | bytes 688136 | tf_op jit(solution)/shard_map/ppermute | solution.py:29
  45.9 19.6 %copy-start.21 = (bf16[112,1024]{1,0:T(8,128)(2,1)}, bf16[112,1024]{1,0:T(8,128)(2,1)S(1)}, u32[]{:S(2)}) copy-start(bf16[112,1024]{1,0:T(8,128)(2,1)S(1)} %collective-permute-done.4.refs_2_) | copy-start | bytes 688132
  49.9 15.6 %copy-start.22 = (bf16[112,1024]{1,0:T(8,128)(2,1)}, bf16[112,1024]{1,0:T(8,128)(2,1)S(1)}, u32[]{:S(2)}) copy-start(bf16[112,1024]{1,0:T(8,128)(2,1)S(1)} %collective-permute-done.6.refs_6_) | copy-start | bytes 688132
  50.0 15.5 %collective-permute-start.11 = (bf16[512,1024]{1,0:T(8,128)(2,1)}, bf16[512,1024]{1,0:T(8,128)(2,1)}, u32[]{:S(2)}, u32[]{:S(2)}) collective-permute-start(bf16[512,1024]{1,0:T(8,128)(2,1)} %collective-permute-done.2.refs_9_), channel_id=1, source_target_pairs={{0,1},{1,0},{2,3},{3,2},{4,5},{5,4},{6,7},{7,6},{8,9},{9,8},{10,11... | collective-permute-start | bytes 3145736 | tf_op jit(solution)/shard_map/ppermute | solution.py:29
  51.5 13.9 %collective-permute-start.12 = (bf16[512,1024]{1,0:T(8,128)(2,1)}, bf16[512,1024]{1,0:T(8,128)(2,1)}, u32[]{:S(2)}, u32[]{:S(2)}) collective-permute-start(bf16[512,1024]{1,0:T(8,128)(2,1)} %collective-permute-done.3.refs_10_), channel_id=1, source_target_pairs={{0,1},{1,0},{2,3},{3,2},{4,5},{5,4},{6,7},{7,6},{8,9},{9,8},{10,11... | collective-permute-start | bytes 3145736 | tf_op jit(solution)/shard_map/ppermute | solution.py:29
  52.2 25.8 %collective-permute-start.13 = (bf16[512,1024]{1,0:T(8,128)(2,1)}, bf16[512,1024]{1,0:T(8,128)(2,1)S(1)}, u32[]{:S(2)}, u32[]{:S(2)}) collective-permute-start(bf16[512,1024]{1,0:T(8,128)(2,1)} %collective-permute-done.2.refs_9_), channel_id=1, source_target_pairs={{0,64},{1,65},{2,66},{3,67},{4,68},{5,69},{6,70},{7,71},{8,72},{9,... | collective-permute-start | bytes 3145736 | tf_op jit(solution)/shard_map/ppermute | solution.py:29
  52.3 7.0 %collective-permute-start.8 = (bf16[112,1024]{1,0:T(8,128)(2,1)S(1)}, bf16[112,1024]{1,0:T(8,128)(2,1)}, u32[]{:S(2)}, u32[]{:S(2)}) collective-permute-start(bf16[112,1024]{1,0:T(8,128)(2,1)S(1)} %collective-permute-done.4.refs_2_), channel_id=1, source_target_pairs={{0,8},{1,9},{2,10},{3,11},{4,12},{5,13},{6,14},{7,15},{8,16},{9,17... | collective-permute-start | bytes 688136 | tf_op jit(solution)/shard_map/ppermute | solution.py:29
  54.6 7.8 %collective-permute-start.10 = (bf16[112,1024]{1,0:T(8,128)(2,1)S(1)}, bf16[112,1024]{1,0:T(8,128)(2,1)}, u32[]{:S(2)}, u32[]{:S(2)}) collective-permute-start(bf16[112,1024]{1,0:T(8,128)(2,1)S(1)} %collective-permute-done.6.refs_6_), channel_id=1, source_target_pairs={{0,56},{1,57},{2,58},{3,59},{4,60},{5,61},{6,62},{7,63},{8,0},{9,1... | collective-permute-start | bytes 688136 | tf_op jit(solution)/shard_map/ppermute | solution.py:29
  59.3 6.2 %collective-permute-start.9 = (bf16[112,1024]{1,0:T(8,128)(2,1)}, bf16[112,1024]{1,0:T(8,128)(2,1)}, u32[]{:S(2)}, u32[]{:S(2)}) collective-permute-start(bf16[112,1024]{1,0:T(8,128)(2,1)} %collective-permute-done.8.refs_3_), channel_id=1, source_target_pairs={{0,8},{1,9},{2,10},{3,11},{4,12},{5,13},{6,14},{7,15},{8,16},{9,17... | collective-permute-start | bytes 688136 | tf_op jit(solution)/shard_map/ppermute | solution.py:29
  78.0 8.4 %collective-permute-start.17 = (bf16[512,1024]{1,0:T(8,128)(2,1)S(1)}, bf16[512,1024]{1,0:T(8,128)(2,1)S(1)}, u32[]{:S(2)}, u32[]{:S(2)}) collective-permute-start(bf16[512,1024]{1,0:T(8,128)(2,1)S(1)} %collective-permute-done.13.refs_8_), channel_id=1, source_target_pairs={{0,1},{1,0},{2,3},{3,2},{4,5},{5,4},{6,7},{7,6},{8,9},{9,8},{10,11... | collective-permute-start | bytes 3145736 | tf_op jit(solution)/shard_map/ppermute | solution.py:29
  79.3 13.0 %copy-start.28 = (s32[4]{0:T(128)}, s32[4]{0:T(128)S(1)}, u32[]{:S(2)}) copy-start(s32[4]{0:T(128)S(1)} %get-tuple-element.76.xs) | copy-start | bytes 52
  79.6 13.4 %collective-permute-start.14 = (bf16[112,1536]{1,0:T(8,128)(2,1)}, bf16[112,1536]{1,0:T(8,128)(2,1)S(1)}, u32[]{:S(2)}, u32[]{:S(2)}) collective-permute-start(bf16[112,1536]{1,0:T(8,128)(2,1)} %get-tuple-element.55), channel_id=1, source_target_pairs={{0,4},{1,5},{2,6},{3,7},{4,0},{5,1},{6,2},{7,3},{8,12},{9,13},{10,... | collective-permute-start | bytes 1032200 | tf_op jit(solution)/shard_map/ppermute | solution.py:29
  82.6 16.4 %collective-permute-start.15 = (bf16[112,1536]{1,0:T(8,128)(2,1)}, bf16[112,1536]{1,0:T(8,128)(2,1)S(1)}, u32[]{:S(2)}, u32[]{:S(2)}) collective-permute-start(bf16[112,1536]{1,0:T(8,128)(2,1)} %get-tuple-element.56), channel_id=1, source_target_pairs={{0,2},{1,3},{2,4},{3,5},{4,6},{5,7},{6,0},{7,1},{8,10},{9,11},{10,... | collective-permute-start | bytes 1032200 | tf_op jit(solution)/shard_map/ppermute | solution.py:29
  83.1 15.9 %collective-permute-start.16 = (bf16[112,1536]{1,0:T(8,128)(2,1)}, bf16[112,1536]{1,0:T(8,128)(2,1)S(1)}, u32[]{:S(2)}, u32[]{:S(2)}) collective-permute-start(bf16[112,1536]{1,0:T(8,128)(2,1)} %get-tuple-element.57), channel_id=1, source_target_pairs={{0,6},{1,7},{2,0},{3,1},{4,2},{5,3},{6,4},{7,5},{8,14},{9,15},{10,... | collective-permute-start | bytes 1032200 | tf_op jit(solution)/shard_map/ppermute | solution.py:29
  92.3 8.6 %collective-permute-start.18 = (bf16[112,512]{1,0:T(8,128)(2,1)}, bf16[112,512]{1,0:T(8,128)(2,1)S(1)}, u32[]{:S(2)}, u32[]{:S(2)}) collective-permute-start(bf16[112,512]{1,0:T(8,128)(2,1)} %get-tuple-element.60), channel_id=1, source_target_pairs={{0,4},{1,5},{2,6},{3,7},{4,0},{5,1},{6,2},{7,3},{8,12},{9,13},{10,... | collective-permute-start | bytes 344072 | tf_op jit(solution)/shard_map/ppermute | solution.py:29
  92.4 11.2 %collective-permute-start.19 = (bf16[112,512]{1,0:T(8,128)(2,1)}, bf16[112,512]{1,0:T(8,128)(2,1)S(1)}, u32[]{:S(2)}, u32[]{:S(2)}) collective-permute-start(bf16[112,512]{1,0:T(8,128)(2,1)} %get-tuple-element.61), channel_id=1, source_target_pairs={{0,2},{1,3},{2,4},{3,5},{4,6},{5,7},{6,0},{7,1},{8,10},{9,11},{10,... | collective-permute-start | bytes 344072 | tf_op jit(solution)/shard_map/ppermute | solution.py:29
  93.0 10.8 %copy-start.15 = (bf16[112,1536]{1,0:T(8,128)(2,1)}, bf16[112,1536]{1,0:T(8,128)(2,1)S(1)}, u32[]{:S(2)}) copy-start(bf16[112,1536]{1,0:T(8,128)(2,1)S(1)} %collective-permute-done.14.refs_1_) | copy-start | bytes 1032196
  93.0 10.8 %collective-permute-start.20 = (bf16[112,512]{1,0:T(8,128)(2,1)}, bf16[112,512]{1,0:T(8,128)(2,1)S(1)}, u32[]{:S(2)}, u32[]{:S(2)}) collective-permute-start(bf16[112,512]{1,0:T(8,128)(2,1)} %get-tuple-element.62), channel_id=1, source_target_pairs={{0,6},{1,7},{2,0},{3,1},{4,2},{5,3},{6,4},{7,5},{8,14},{9,15},{10,... | collective-permute-start | bytes 344072 | tf_op jit(solution)/shard_map/ppermute | solution.py:29
  104.4 11.1 %copy-start.29 = (bf16[448]{0:T(512)(128)(2,1)S(1)}, bf16[448]{0:T(512)(128)(2,1)}, u32[]{:S(2)}) copy-start(bf16[448]{0:T(512)(128)(2,1)} %param.21) | copy-start | bytes 2692
  104.4 11.1 %copy-start.30 = (bf16[448]{0:T(512)(128)(2,1)S(1)}, bf16[448]{0:T(512)(128)(2,1)}, u32[]{:S(2)}) copy-start(bf16[448]{0:T(512)(128)(2,1)} %param.22) | copy-start | bytes 2692
  108.6 8.5 %copy-start.4 = (bf16[512,896]{1,0:T(8,128)(2,1)S(1)}, bf16[512,896]{1,0:T(8,128)(2,1)}, u32[]{:S(2)}) copy-start(bf16[512,896]{1,0:T(8,128)(2,1)} %param.23) | copy-start | bytes 2752516
  108.6 8.5 %copy-start.5 = (bf16[512,896]{1,0:T(8,128)(2,1)S(1)}, bf16[512,896]{1,0:T(8,128)(2,1)}, u32[]{:S(2)}) copy-start(bf16[512,896]{1,0:T(8,128)(2,1)} %param.24) | copy-start | bytes 2752516
  108.6 41.5 %all-to-all-start = ((bf16[32,112,128]{2,1,0:T(8,128)(2,1)}), bf16[32,112,128]{2,1,0:T(8,128)(2,1)S(1)}, u32[]{:S(2)}, u32[]{:S(2)}) async-start(bf16[32,112,128]{2,1,0:T(8,128)(2,1)} %send.1), calls=%async_computation | async-start | bytes 1835008 | tf_op jit(solution)/shard_map/all_to_all | solution.py:366
  127.9 52.7 %copy-start.31 = (s32[8]{0:T(128)S(1)}, s32[8]{0:T(128)}, u32[]{:S(2)}) copy-start(s32[8]{0:T(128)} %constant.211.clone) | copy-start | bytes 100
  154.4 11.6 %collective-permute-start.22 = (bf16[464,512]{1,0:T(8,128)(2,1)}, bf16[464,512]{1,0:T(8,128)(2,1)S(1)}, u32[]{:S(2)}, u32[]{:S(2)}) collective-permute-start(bf16[464,512]{1,0:T(8,128)(2,1)} %recv.1.refs_0_), channel_id=1, source_target_pairs={{0,2},{1,3},{2,4},{3,5},{4,6},{5,7},{6,0},{7,1},{8,10},{9,11},{10,... | collective-permute-start | bytes 1425416 | tf_op jit(solution)/shard_map/ppermute | solution.py:29
  155.6 14.8 %collective-permute-start.24 = (bf16[464,512]{1,0:T(8,128)(2,1)}, bf16[464,512]{1,0:T(8,128)(2,1)S(1)}, u32[]{:S(2)}, u32[]{:S(2)}) collective-permute-start(bf16[464,512]{1,0:T(8,128)(2,1)} %recv.1.refs_0_), channel_id=1, source_target_pairs={{0,6},{1,7},{2,0},{3,1},{4,2},{5,3},{6,4},{7,5},{8,14},{9,15},{10,... | collective-permute-start | bytes 1425416 | tf_op jit(solution)/shard_map/ppermute | solution.py:29
  157.1 21.6 %collective-permute-start.26 = (bf16[464,512]{1,0:T(8,128)(2,1)}, bf16[464,512]{1,0:T(8,128)(2,1)S(1)}, u32[]{:S(2)}, u32[]{:S(2)}) collective-permute-start(bf16[464,512]{1,0:T(8,128)(2,1)} %recv.1.refs_0_), channel_id=1, source_target_pairs={{0,4},{1,5},{2,6},{3,7},{4,0},{5,1},{6,2},{7,3},{8,12},{9,13},{10,... | collective-permute-start | bytes 1425416 | tf_op jit(solution)/shard_map/ppermute | solution.py:29
  158.3 22.9 %collective-permute-start.21 = (bf16[464,512]{1,0:T(8,128)(2,1)}, bf16[464,512]{1,0:T(8,128)(2,1)S(1)}, u32[]{:S(2)}, u32[]{:S(2)}) collective-permute-start(bf16[464,512]{1,0:T(8,128)(2,1)} %recv.1.refs_0_), channel_id=1, source_target_pairs={{0,1},{1,0},{2,3},{3,2},{4,5},{5,4},{6,7},{7,6},{8,9},{9,8},{10,11... | collective-permute-start | bytes 1425416 | tf_op jit(solution)/shard_map/ppermute | solution.py:29
  166.0 15.9 %copy-start.8 = (bf16[464,512]{1,0:T(8,128)(2,1)}, bf16[464,512]{1,0:T(8,128)(2,1)S(1)}, u32[]{:S(2)}) copy-start(bf16[464,512]{1,0:T(8,128)(2,1)S(1)} %collective-permute-done.22.refs_2_) | copy-start | bytes 1425412
  166.0 15.2 %collective-permute-start.23 = (bf16[464,512]{1,0:T(8,128)(2,1)S(1)}, bf16[464,512]{1,0:T(8,128)(2,1)S(1)}, u32[]{:S(2)}, u32[]{:S(2)}) collective-permute-start(bf16[464,512]{1,0:T(8,128)(2,1)S(1)} %collective-permute-done.22.refs_2_), channel_id=1, source_target_pairs={{0,1},{1,0},{2,3},{3,2},{4,5},{5,4},{6,7},{7,6},{8,9},{9,8},{10,11... | collective-permute-start | bytes 1425416 | tf_op jit(solution)/shard_map/ppermute | solution.py:29
  170.4 11.6 %copy-start.9 = (bf16[464,512]{1,0:T(8,128)(2,1)}, bf16[464,512]{1,0:T(8,128)(2,1)S(1)}, u32[]{:S(2)}) copy-start(bf16[464,512]{1,0:T(8,128)(2,1)S(1)} %collective-permute-done.24.refs_4_) | copy-start | bytes 1425412
  170.4 10.9 %collective-permute-start.25 = (bf16[464,512]{1,0:T(8,128)(2,1)S(1)}, bf16[464,512]{1,0:T(8,128)(2,1)S(1)}, u32[]{:S(2)}, u32[]{:S(2)}) collective-permute-start(bf16[464,512]{1,0:T(8,128)(2,1)S(1)} %collective-permute-done.24.refs_4_), channel_id=1, source_target_pairs={{0,1},{1,0},{2,3},{3,2},{4,5},{5,4},{6,7},{7,6},{8,9},{9,8},{10,11... | collective-permute-start | bytes 1425416 | tf_op jit(solution)/shard_map/ppermute | solution.py:29
  178.7 3.2 %collective-permute-start.27 = (bf16[464,512]{1,0:T(8,128)(2,1)S(1)}, bf16[464,512]{1,0:T(8,128)(2,1)S(1)}, u32[]{:S(2)}, u32[]{:S(2)}) collective-permute-start(bf16[464,512]{1,0:T(8,128)(2,1)S(1)} %collective-permute-done.26.refs_6_), channel_id=1, source_target_pairs={{0,1},{1,0},{2,3},{3,2},{4,5},{5,4},{6,7},{7,6},{8,9},{9,8},{10,11... | collective-permute-start | bytes 1425416 | tf_op jit(solution)/shard_map/ppermute | solution.py:29
  (18 other events, 44.0 us)
Sparse Core Ops, SparseCore 0:
  11.0 51.4 all-gather.2
  65.1 102.6 all-gather.4

commit v2 on v1

--- a/solution.py
+++ b/solution.py
@@ -202,6 +202,7 @@
     copies.append(pltpu.make_async_copy(active, scale_buf.at[1], sems.at[25]))
     for copy in copies:
         copy.start()
+    value[...] = jnp.zeros((512, 896), F32)
     for copy in copies[:9]:
         copy.wait()
     out_scale, resid_scale, pull, push = row_factors(stat_buf, grad_buf)
@@ -223,7 +224,6 @@
     total, post = totals(0)
     resid_grad[...] = total.astype(BF)
     even[...] = post
-    value[...] = jnp.zeros((512, 896), F32)
 
     @pl.loop(0, 4)
     def _(pair):

time: 204 us -> 204 us (level)
  no operation moved by 1% of the time
where the time goes in v2:
time: 204 us; the launch traced here: 203 us
  waiting for transfers between devices  71.1 us (35%)
  starting transfers between devices  58.5 us (29%)
  Pallas kernels  41 us (20%)
  between operations  14.6 us (7%)
  other arithmetic  9.24 us (5%)
  local copies, waits for them, and re-layouts  9.01 us (4%)
    ppermute x27, starting transfers between devices, move(): return lax.ppermute(value, AXES, pairs)  44.5 us
    ppermute x27, waiting for transfers between devices, move(): return lax.ppermute(value, AXES, pairs)  39.9 us
    all_to_all x1, waiting for transfers between devices, per_device(): arrived = lax.all_to_all(outgoing, 'dp', 0, 0, tiled=True)  22.2 us
    pallas_call x1, Pallas kernels, per_device(): call(final_kernel, (jax.ShapeDtypeStruct((448, 512), BF), jax.ShapeDtypeS...  13.4 us
    pallas_call x2, Pallas kernels, part(): call(part_kernel, (jax.ShapeDtypeStruct((112, size), BF),) * 4, 2, 8 + 2...  12.4 us
    ppermute x1, waiting for transfers between devices, spread_columns(): return lax.ppermute(shard, AXES, pairs)  8.97 us
    pallas_call x1, Pallas kernels, per_device(): call(stats_kernel, jax.ShapeDtypeStruct((8, 512), F32), 0, 1, 3584 * 512...  7.64 us
    ppermute x1, starting transfers between devices, spread_columns(): return lax.ppermute(shard, AXES, pairs)  7.06 us
  transfers between devices with their start and end apart: 31, of which 16 were waited for; matrix products, arithmetic and copies ran while one was open for 5% of the time, Pallas kernels for 10%

profile of v2, /device:TPU:33, one launch (start us, length us, event | category | flops | bytes accessed | tf_op | source)
XLA Modules:
  0.0 203.4 jit_solution(947759089553031759)
XLA Ops:
  8.7 2.2 %pad_maximum_fusion.1 = bf16[912,512]{1,0:T(8,128)(2,1)} fusion(bf16[16,512]{1,0:T(8,128)(2,1)S(1)} %fusion.14, bf16[448,512]{1,0:T(8,128)(2,1)} %bitcast.33, bf16[448,512]{1,0:T(8,128)(2,1)} %bitcast.31), kind=kLoop, calls=%fused_computation.16 | loop fusion | flops 2801664 | bytes 1867776 | tf_op jit(solution)/shard_map/concatenate | solution.py:308
  11.1 0.8 copy-done.7
  12.1 1.3 collective-permute-start.2
  13.4 1.5 collective-permute-start.3
  14.9 1.2 collective-permute-start.7
  16.1 7.1 %collective-permute-start = (bf16[112,1024]{1,0:T(8,128)(2,1)S(1)}, bf16[112,1024]{1,0:T(8,128)(2,1)S(1)}, u32[]{:S(2)}, u32[]{:S(2)}) collective-permute-start(bf16[112,1024]{1,0:T(8,128)(2,1)S(1)} %pad_maximum_fusion.2), channel_id=1, source_target_pairs={{0,0},{1,32},{2,2},{3,34},{4,4},{5,36},{6,6},{7,38},{8,64},{9,96},... | collective-permute-start | bytes 688136 | tf_op jit(solution)/shard_map/ppermute | solution.py:41
  23.2 9.0 %collective-permute-done.refs_0_ = bf16[112,1024]{1,0:T(8,128)(2,1)S(1)} collective-permute-done((bf16[112,1024]{1,0:T(8,128)(2,1)S(1)}, bf16[112,1024]{1,0:T(8,128)(2,1)S(1)}, u32[]{:S(2)}, u32[]{:S(2)}) %collective-permute-start) | collective-permute-done | bytes 229408 | tf_op jit(solution)/shard_map/ppermute | solution.py:41
  32.7 0.9 collective-permute-start.5
  33.6 3.8 %collective-permute-done.1.refs_1_ = bf16[112,1024]{1,0:T(8,128)(2,1)S(1)} collective-permute-done((bf16[112,1024]{1,0:T(8,128)(2,1)S(1)}, bf16[112,1024]{1,0:T(8,128)(2,1)S(1)}, u32[]{:S(2)}, u32[]{:S(2)}) %collective-permute-start.1) | collective-permute-done | bytes 229408 | tf_op jit(solution)/shard_map/ppermute | solution.py:29
  37.4 3.9 %collective-permute-start.4 = (bf16[112,1024]{1,0:T(8,128)(2,1)S(1)}, bf16[112,1024]{1,0:T(8,128)(2,1)S(1)}, u32[]{:S(2)}, u32[]{:S(2)}) collective-permute-start(bf16[112,1024]{1,0:T(8,128)(2,1)S(1)} %collective-permute-done.1.refs_1_), channel_id=1, source_target_pairs={{0,8},{1,9},{2,10},{3,11},{4,12},{5,13},{6,14},{7,15},{8,16},{9,17... | collective-permute-start | bytes 688136 | tf_op jit(solution)/shard_map/ppermute | solution.py:29
  41.3 2.0 collective-permute-done.5.refs_5_
  43.3 2.5 %collective-permute-done.4.refs_2_ = bf16[112,1024]{1,0:T(8,128)(2,1)S(1)} collective-permute-done((bf16[112,1024]{1,0:T(8,128)(2,1)S(1)}, bf16[112,1024]{1,0:T(8,128)(2,1)S(1)}, u32[]{:S(2)}, u32[]{:S(2)}) %collective-permute-start.4) | collective-permute-done | bytes 229408 | tf_op jit(solution)/shard_map/ppermute | solution.py:29
  45.9 4.0 %collective-permute-done.6.refs_6_ = bf16[112,1024]{1,0:T(8,128)(2,1)S(1)} collective-permute-done((bf16[112,1024]{1,0:T(8,128)(2,1)S(1)}, bf16[112,1024]{1,0:T(8,128)(2,1)S(1)}, u32[]{:S(2)}, u32[]{:S(2)}) %collective-permute-start.6) | collective-permute-done | bytes 229408 | tf_op jit(solution)/shard_map/ppermute | solution.py:29
  50.0 1.5 collective-permute-start.11
  52.3 1.5 collective-permute-start.8
  54.7 4.5 %collective-permute-done.8.refs_3_ = bf16[112,1024]{1,0:T(8,128)(2,1)} collective-permute-done((bf16[112,1024]{1,0:T(8,128)(2,1)S(1)}, bf16[112,1024]{1,0:T(8,128)(2,1)}, u32[]{:S(2)}, u32[]{:S(2)}) %collective-permute-start.8) | collective-permute-done | bytes 229408 | tf_op jit(solution)/shard_map/ppermute | solution.py:29
  59.3 1.4 collective-permute-start.9
  61.5 0.9 collective-permute-done.10.refs_7_
  62.4 3.0 %collective-permute-done.9.refs_4_ = bf16[112,1024]{1,0:T(8,128)(2,1)} collective-permute-done((bf16[112,1024]{1,0:T(8,128)(2,1)}, bf16[112,1024]{1,0:T(8,128)(2,1)}, u32[]{:S(2)}, u32[]{:S(2)}) %collective-permute-start.9) | collective-permute-done | bytes 229408 | tf_op jit(solution)/shard_map/ppermute | solution.py:29
  65.5 7.5 %part.2 = (bf16[112,1536]{1,0:T(8,128)(2,1)}, bf16[112,1536]{1,0:T(8,128)(2,1)}, bf16[112,1536]{1,0:T(8,128)(2,1)}, bf16[112,1536]{1,0:T(8,128)(2,1)}) custom-call(s32[8]{0:T(128)} %fusion.25.where, s32[1]{0:T(128)} %bitcast.12.core, bf16[112,1024]{1,0:T(8,128)(2,1)} %copy-done.18, bf16[112,1024]{1,0:T(8,128)(2,1)} %copy-done.19, ...), custom_call_target="tpu_custom_call" | custom-call | flops 2818572288 | bytes 6000000 | tf_op jit(solution)/shard_map/part/pallas_call | solution.py:333
  73.0 5.0 %collective-permute-done.13.refs_8_ = bf16[512,1024]{1,0:T(8,128)(2,1)S(1)} collective-permute-done((bf16[512,1024]{1,0:T(8,128)(2,1)}, bf16[512,1024]{1,0:T(8,128)(2,1)S(1)}, u32[]{:S(2)}, u32[]{:S(2)}) %collective-permute-start.13) | collective-permute-done | bytes 1048608 | tf_op jit(solution)/shard_map/ppermute | solution.py:29
  78.0 1.2 collective-permute-start.17
  79.6 2.9 %collective-permute-start.14 = (bf16[112,1536]{1,0:T(8,128)(2,1)}, bf16[112,1536]{1,0:T(8,128)(2,1)S(1)}, u32[]{:S(2)}, u32[]{:S(2)}) collective-permute-start(bf16[112,1536]{1,0:T(8,128)(2,1)} %get-tuple-element.55), channel_id=1, source_target_pairs={{0,4},{1,5},{2,6},{3,7},{4,0},{5,1},{6,2},{7,3},{8,12},{9,13},{10,... | collective-permute-start | bytes 1032200 | tf_op jit(solution)/shard_map/ppermute | solution.py:29
  83.1 2.3 %collective-permute-start.16 = (bf16[112,1536]{1,0:T(8,128)(2,1)}, bf16[112,1536]{1,0:T(8,128)(2,1)S(1)}, u32[]{:S(2)}, u32[]{:S(2)}) collective-permute-start(bf16[112,1536]{1,0:T(8,128)(2,1)} %get-tuple-element.57), channel_id=1, source_target_pairs={{0,6},{1,7},{2,0},{3,1},{4,2},{5,3},{6,4},{7,5},{8,14},{9,15},{10,... | collective-permute-start | bytes 1032200 | tf_op jit(solution)/shard_map/ppermute | solution.py:29
  86.4 1.0 copy-done.2
  87.4 4.9 %part.3 = (bf16[112,512]{1,0:T(8,128)(2,1)}, bf16[112,512]{1,0:T(8,128)(2,1)}, bf16[112,512]{1,0:T(8,128)(2,1)}, bf16[112,512]{1,0:T(8,128)(2,1)}) custom-call(s32[8]{0:T(128)} %fusion.25.where, s32[1]{0:T(128)} %bitcast.12.core, bf16[112,1024]{1,0:T(8,128)(2,1)} %copy-done.18, bf16[112,1024]{1,0:T(8,128)(2,1)} %copy-done.19, bf16[112,1024]{1,0:T(8,128)(2,1)} %copy-done.21, ...), custom_call_target="tpu_custom_call" | custom-call | flops 939524096 | bytes 6000000 | tf_op jit(solution)/shard_map/part/pallas_call | solution.py:333
  93.0 2.2 %collective-permute-start.20 = (bf16[112,512]{1,0:T(8,128)(2,1)}, bf16[112,512]{1,0:T(8,128)(2,1)S(1)}, u32[]{:S(2)}, u32[]{:S(2)}) collective-permute-start(bf16[112,512]{1,0:T(8,128)(2,1)} %get-tuple-element.62), channel_id=1, source_target_pairs={{0,6},{1,7},{2,0},{3,1},{4,2},{5,3},{6,4},{7,5},{8,14},{9,15},{10,... | collective-permute-start | bytes 344072 | tf_op jit(solution)/shard_map/ppermute | solution.py:29
  95.8 3.2 %collective-permute-done.15.refs_2_ = bf16[112,1536]{1,0:T(8,128)(2,1)S(1)} collective-permute-done((bf16[112,1536]{1,0:T(8,128)(2,1)}, bf16[112,1536]{1,0:T(8,128)(2,1)S(1)}, u32[]{:S(2)}, u32[]{:S(2)}) %collective-permute-start.15) | collective-permute-done | bytes 344096 | tf_op jit(solution)/shard_map/ppermute | solution.py:29
  99.0 1.9 collective-permute-done.18.refs_5_
  100.9 2.7 %collective-permute-done.19.refs_6_ = bf16[112,512]{1,0:T(8,128)(2,1)S(1)} collective-permute-done((bf16[112,512]{1,0:T(8,128)(2,1)}, bf16[112,512]{1,0:T(8,128)(2,1)S(1)}, u32[]{:S(2)}, u32[]{:S(2)}) %collective-permute-start.19) | collective-permute-done | bytes 114720 | tf_op jit(solution)/shard_map/ppermute | solution.py:29
  104.4 4.3 %send.1 = bf16[32,112,128]{2,1,0:T(8,128)(2,1)} custom-call(s32[4]{0:T(128)} %copy-done.28, bf16[112,1536]{1,0:T(8,128)(2,1)} %get-tuple-element.54.refs_0_, bf16[112,1536]{1,0:T(8,128)(2,1)} %copy-done.15, bf16[112,1536]{1,0:T(8,128)(2,1)} %copy-done.16, bf16[112,1536]{1,0:T(8,128)(2,1)} %copy-done.17, bf16[112,512]{1,0:T(8,128)(2,1)} %get-tuple-element.59.refs_4_, ...), custom_call_target="tpu_custom_call" | custom-call | flops 469762048 | bytes 6000000 | tf_op jit(solution)/shard_map/send/pallas_call | solution.py:357
  108.6 6.8 %all-to-all-start = ((bf16[32,112,128]{2,1,0:T(8,128)(2,1)}), bf16[32,112,128]{2,1,0:T(8,128)(2,1)S(1)}, u32[]{:S(2)}, u32[]{:S(2)}) async-start(bf16[32,112,128]{2,1,0:T(8,128)(2,1)} %send.1), calls=%async_computation | async-start | bytes 1835008 | tf_op jit(solution)/shard_map/all_to_all | solution.py:366
  115.5 0.8 copy.19.gain_post
  116.3 0.8 copy.20.gain_final
  117.2 3.1 %fusion.3 = (f32[512,896]{1,0:T(8,128)}, f32[512,896]{1,0:T(8,128)}) fusion(bf16[512,896]{1,0:T(8,128)(2,1)S(1)} %copy-done.4, bf16[512,896]{1,0:T(8,128)(2,1)S(1)} %copy-done.5), kind=kLoop, calls=%fused_computation.10 | loop fusion | flops 9633792 | bytes 5505024 | tf_op jit(solution)/shard_map/mul | solution.py:323
  120.3 7.6 %stats.1.refs_12_ = f32[8,512]{1,0:T(8,128)} custom-call(bf16[7296,512]{1,0:T(8,128)(2,1)} %all-gather.3.cloned.1.call-done.bundle.refs_9_), custom_call_target="tpu_custom_call" | custom-call | flops 22020096 | bytes 6000000 | tf_op jit(solution)/shard_map/stats/pallas_call | solution.py:367
  127.9 22.2 %all-to-all-done.arrived = bf16[32,112,128]{2,1,0:T(8,128)(2,1)S(1)} async-done(((bf16[32,112,128]{2,1,0:T(8,128)(2,1)}), bf16[32,112,128]{2,1,0:T(8,128)(2,1)S(1)}, u32[]{:S(2)}, u32[]{:S(2)}) %all-to-all-start) | async-done | bytes 917536 | tf_op jit(solution)/shard_map/all_to_all | solution.py:366
  150.2 0.9 copy-done
  151.1 3.3 %recv.1.refs_0_ = bf16[464,512]{1,0:T(8,128)(2,1)} custom-call(bf16[32,112,128]{2,1,0:T(8,128)(2,1)} %copy-done, s32[1,512]{1,0:T(1,128)} %add.273.row_pos, bf16[448,512]{1,0:T(8,128)(2,1)} %bitcast.32, bf16[448,512]{1,0:T(8,128)(2,1)} %bitcast.34, f32[448,1]{1,0:T(8,128)} %copy.19.gain_post, f32[448,1]{1,0:T(8,128)} %copy.20.gain_final, f32[8,512]{1,0:T(8,128)} %stats.1.refs_12_), custom_call_target="tpu_custom_call" | custom-call | flops 469762048 | bytes 6000000 | tf_op jit(solution)/shard_map/recv/pallas_call | solution.py:379
  154.4 1.2 collective-permute-start.22
  155.6 1.5 collective-permute-start.24
  157.1 1.2 collective-permute-start.26
  158.3 2.4 %collective-permute-start.21 = (bf16[464,512]{1,0:T(8,128)(2,1)}, bf16[464,512]{1,0:T(8,128)(2,1)S(1)}, u32[]{:S(2)}, u32[]{:S(2)}) collective-permute-start(bf16[464,512]{1,0:T(8,128)(2,1)} %recv.1.refs_0_), channel_id=1, source_target_pairs={{0,1},{1,0},{2,3},{3,2},{4,5},{5,4},{6,7},{7,6},{8,9},{9,8},{10,11... | collective-permute-start | bytes 1425416 | tf_op jit(solution)/shard_map/ppermute | solution.py:29
  160.7 5.3 %collective-permute-done.22.refs_2_ = bf16[464,512]{1,0:T(8,128)(2,1)S(1)} collective-permute-done((bf16[464,512]{1,0:T(8,128)(2,1)}, bf16[464,512]{1,0:T(8,128)(2,1)S(1)}, u32[]{:S(2)}, u32[]{:S(2)}) %collective-permute-start.22) | collective-permute-done | bytes 475168 | tf_op jit(solution)/shard_map/ppermute | solution.py:29
  166.0 4.3 %collective-permute-start.23 = (bf16[464,512]{1,0:T(8,128)(2,1)S(1)}, bf16[464,512]{1,0:T(8,128)(2,1)S(1)}, u32[]{:S(2)}, u32[]{:S(2)}) collective-permute-start(bf16[464,512]{1,0:T(8,128)(2,1)S(1)} %collective-permute-done.22.refs_2_), channel_id=1, source_target_pairs={{0,1},{1,0},{2,3},{3,2},{4,5},{5,4},{6,7},{7,6},{8,9},{9,8},{10,11... | collective-permute-start | bytes 1425416 | tf_op jit(solution)/shard_map/ppermute | solution.py:29
  170.4 8.4 %collective-permute-start.25 = (bf16[464,512]{1,0:T(8,128)(2,1)S(1)}, bf16[464,512]{1,0:T(8,128)(2,1)S(1)}, u32[]{:S(2)}, u32[]{:S(2)}) collective-permute-start(bf16[464,512]{1,0:T(8,128)(2,1)S(1)} %collective-permute-done.24.refs_4_), channel_id=1, source_target_pairs={{0,1},{1,0},{2,3},{3,2},{4,5},{5,4},{6,7},{7,6},{8,9},{9,8},{10,11... | collective-permute-start | bytes 1425416 | tf_op jit(solution)/shard_map/ppermute | solution.py:29
  178.7 1.8 collective-permute-start.27
  183.1 13.4 %final.1 = (bf16[448,512]{1,0:T(8,128)(2,1)}, bf16[512,896]{1,0:T(8,128)(2,1)}, bf16[512,896]{1,0:T(8,128)(2,1)}) custom-call(s32[8]{0:T(128)} %fusion.24.heads, bf16[464,512]{1,0:T(8,128)(2,1)} %recv.1.refs_0_, bf16[464,512]{1,0:T(8,128)(2,1)} %copy-done.11, bf16[464,512]{1,0:T(8,128)(2,1)} %copy-done.8, bf16[464,512]{1,0:T(8,128)(2,1)} %copy-done.12, ...), custom_call_target="tpu_custom_call" | custom-call | flops 3288334336 | bytes 6000000 | tf_op jit(solution)/shard_map/final/pallas_call | solution.py:393
  (130 shorter events, 11.4 us)
Async XLA Ops:
  7.2 113.1 %all-gather.3.cloned.1.call-start = ((), (), s32[]{:S(2)}) async-start(), calls=%async_computation.1 | async-start | bytes 8404992 | tf_op jit(solution)/shard_map/all_gather | solution.py:309
  10.9 170.3 %all-gather.5.cloned.1.call-start = ((), (), s32[]{:S(2)}) async-start(), calls=%async_computation.2 | async-start | bytes 6623232 | tf_op jit(solution)/shard_map/all_gather | solution.py:325
  11.9 11.3 %copy-start.34 = (s32[8]{0:T(128)S(1)}, s32[8]{0:T(128)}, u32[]{:S(2)}) copy-start(s32[8]{0:T(128)} %constant.217) | copy-start | bytes 100
  11.9 39.7 %copy-start.32 = (s32[1024]{0:T(1024)S(1)}, s32[1024]{0:T(1024)}, u32[]{:S(2)}) copy-start(s32[1024]{0:T(1024)} %param.18) | copy-start | bytes 12292
  12.1 53.4 %copy-start.3 = (bf16[512,1024]{1,0:T(8,128)(2,1)}, bf16[512,1024]{1,0:T(8,128)(2,1)S(1)}, u32[]{:S(2)}) copy-start(bf16[512,1024]{1,0:T(8,128)(2,1)S(1)} %pad_maximum_fusion.refs_8_) | copy-start | bytes 3145732
  12.1 37.8 %collective-permute-start.2 = (bf16[512,1024]{1,0:T(8,128)(2,1)S(1)}, bf16[512,1024]{1,0:T(8,128)(2,1)}, u32[]{:S(2)}, u32[]{:S(2)}) collective-permute-start(bf16[512,1024]{1,0:T(8,128)(2,1)S(1)} %pad_maximum_fusion.refs_8_), channel_id=1, source_target_pairs={{0,64},{1,65},{2,66},{3,67},{4,68},{5,69},{6,70},{7,71},{8,72},{9,... | collective-permute-start | bytes 3145736 | tf_op jit(solution)/shard_map/ppermute | solution.py:29
  13.4 36.5 %collective-permute-start.3 = (bf16[512,1024]{1,0:T(8,128)(2,1)S(1)}, bf16[512,1024]{1,0:T(8,128)(2,1)}, u32[]{:S(2)}, u32[]{:S(2)}) collective-permute-start(bf16[512,1024]{1,0:T(8,128)(2,1)S(1)} %pad_maximum_fusion.refs_8_), channel_id=1, source_target_pairs={{0,192},{1,193},{2,194},{3,195},{4,196},{5,197},{6,198},{7,199},{8... | collective-permute-start | bytes 3145736 | tf_op jit(solution)/shard_map/ppermute | solution.py:29
  14.9 35.1 %collective-permute-start.7 = (bf16[512,1024]{1,0:T(8,128)(2,1)S(1)}, bf16[512,1024]{1,0:T(8,128)(2,1)S(1)}, u32[]{:S(2)}, u32[]{:S(2)}) collective-permute-start(bf16[512,1024]{1,0:T(8,128)(2,1)S(1)} %pad_maximum_fusion.refs_8_), channel_id=1, source_target_pairs={{0,1},{1,0},{2,3},{3,2},{4,5},{5,4},{6,7},{7,6},{8,9},{9,8},{10,11... | collective-permute-start | bytes 3145736 | tf_op jit(solution)/shard_map/ppermute | solution.py:29
  16.1 16.1 %collective-permute-start = (bf16[112,1024]{1,0:T(8,128)(2,1)S(1)}, bf16[112,1024]{1,0:T(8,128)(2,1)S(1)}, u32[]{:S(2)}, u32[]{:S(2)}) collective-permute-start(bf16[112,1024]{1,0:T(8,128)(2,1)S(1)} %pad_maximum_fusion.2), channel_id=1, source_target_pairs={{0,0},{1,32},{2,2},{3,34},{4,4},{5,36},{6,6},{7,38},{8,64},{9,96},... | collective-permute-start | bytes 688136 | tf_op jit(solution)/shard_map/ppermute | solution.py:41
  32.2 33.3 %copy-start.18 = (bf16[112,1024]{1,0:T(8,128)(2,1)}, bf16[112,1024]{1,0:T(8,128)(2,1)S(1)}, u32[]{:S(2)}) copy-start(bf16[112,1024]{1,0:T(8,128)(2,1)S(1)} %collective-permute-done.refs_0_) | copy-start | bytes 688132
  32.2 5.3 %collective-permute-start.1 = (bf16[112,1024]{1,0:T(8,128)(2,1)S(1)}, bf16[112,1024]{1,0:T(8,128)(2,1)S(1)}, u32[]{:S(2)}, u32[]{:S(2)}) collective-permute-start(bf16[112,1024]{1,0:T(8,128)(2,1)S(1)} %collective-permute-done.refs_0_), channel_id=1, source_target_pairs={{0,8},{1,9},{2,10},{3,11},{4,12},{5,13},{6,14},{7,15},{8,16},{9,17... | collective-permute-start | bytes 688136 | tf_op jit(solution)/shard_map/ppermute | solution.py:29
  32.7 10.6 %collective-permute-start.5 = (bf16[112,1024]{1,0:T(8,128)(2,1)S(1)}, bf16[112,1024]{1,0:T(8,128)(2,1)S(1)}, u32[]{:S(2)}, u32[]{:S(2)}) collective-permute-start(bf16[112,1024]{1,0:T(8,128)(2,1)S(1)} %collective-permute-done.refs_0_), channel_id=1, source_target_pairs={{0,56},{1,57},{2,58},{3,59},{4,60},{5,61},{6,62},{7,63},{8,0},{9,1... | collective-permute-start | bytes 688136 | tf_op jit(solution)/shard_map/ppermute | solution.py:29
  37.4 28.0 %copy-start.19 = (bf16[112,1024]{1,0:T(8,128)(2,1)}, bf16[112,1024]{1,0:T(8,128)(2,1)S(1)}, u32[]{:S(2)}) copy-start(bf16[112,1024]{1,0:T(8,128)(2,1)S(1)} %collective-permute-done.1.refs_1_) | copy-start | bytes 688132
  37.4 8.4 %collective-permute-start.4 = (bf16[112,1024]{1,0:T(8,128)(2,1)S(1)}, bf16[112,1024]{1,0:T(8,128)(2,1)S(1)}, u32[]{:S(2)}, u32[]{:S(2)}) collective-permute-start(bf16[112,1024]{1,0:T(8,128)(2,1)S(1)} %collective-permute-done.1.refs_1_), channel_id=1, source_target_pairs={{0,8},{1,9},{2,10},{3,11},{4,12},{5,13},{6,14},{7,15},{8,16},{9,17... | collective-permute-start | bytes 688136 | tf_op jit(solution)/shard_map/ppermute | solution.py:29
  43.3 22.1 %copy-start.20 = (bf16[112,1024]{1,0:T(8,128)(2,1)}, bf16[112,1024]{1,0:T(8,128)(2,1)S(1)}, u32[]{:S(2)}) copy-start(bf16[112,1024]{1,0:T(8,128)(2,1)S(1)} %collective-permute-done.5.refs_5_) | copy-start | bytes 688132
  43.3 6.6 %collective-permute-start.6 = (bf16[112,1024]{1,0:T(8,128)(2,1)S(1)}, bf16[112,1024]{1,0:T(8,128)(2,1)S(1)}, u32[]{:S(2)}, u32[]{:S(2)}) collective-permute-start(bf16[112,1024]{1,0:T(8,128)(2,1)S(1)} %collective-permute-done.5.refs_5_), channel_id=1, source_target_pairs={{0,56},{1,57},{2,58},{3,59},{4,60},{5,61},{6,62},{7,63},{8,0},{9,1... | collective-permute-start | bytes 688136 | tf_op jit(solution)/shard_map/ppermute | solution.py:29
  45.9 19.6 %copy-start.21 = (bf16[112,1024]{1,0:T(8,128)(2,1)}, bf16[112,1024]{1,0:T(8,128)(2,1)S(1)}, u32[]{:S(2)}) copy-start(bf16[112,1024]{1,0:T(8,128)(2,1)S(1)} %collective-permute-done.4.refs_2_) | copy-start | bytes 688132
  49.9 15.6 %copy-start.22 = (bf16[112,1024]{1,0:T(8,128)(2,1)}, bf16[112,1024]{1,0:T(8,128)(2,1)S(1)}, u32[]{:S(2)}) copy-start(bf16[112,1024]{1,0:T(8,128)(2,1)S(1)} %collective-permute-done.6.refs_6_) | copy-start | bytes 688132
  50.0 15.5 %collective-permute-start.11 = (bf16[512,1024]{1,0:T(8,128)(2,1)}, bf16[512,1024]{1,0:T(8,128)(2,1)}, u32[]{:S(2)}, u32[]{:S(2)}) collective-permute-start(bf16[512,1024]{1,0:T(8,128)(2,1)} %collective-permute-done.2.refs_9_), channel_id=1, source_target_pairs={{0,1},{1,0},{2,3},{3,2},{4,5},{5,4},{6,7},{7,6},{8,9},{9,8},{10,11... | collective-permute-start | bytes 3145736 | tf_op jit(solution)/shard_map/ppermute | solution.py:29
  51.5 13.9 %collective-permute-start.12 = (bf16[512,1024]{1,0:T(8,128)(2,1)}, bf16[512,1024]{1,0:T(8,128)(2,1)}, u32[]{:S(2)}, u32[]{:S(2)}) collective-permute-start(bf16[512,1024]{1,0:T(8,128)(2,1)} %collective-permute-done.3.refs_10_), channel_id=1, source_target_pairs={{0,1},{1,0},{2,3},{3,2},{4,5},{5,4},{6,7},{7,6},{8,9},{9,8},{10,11... | collective-permute-start | bytes 3145736 | tf_op jit(solution)/shard_map/ppermute | solution.py:29
  52.2 25.8 %collective-permute-start.13 = (bf16[512,1024]{1,0:T(8,128)(2,1)}, bf16[512,1024]{1,0:T(8,128)(2,1)S(1)}, u32[]{:S(2)}, u32[]{:S(2)}) collective-permute-start(bf16[512,1024]{1,0:T(8,128)(2,1)} %collective-permute-done.2.refs_9_), channel_id=1, source_target_pairs={{0,64},{1,65},{2,66},{3,67},{4,68},{5,69},{6,70},{7,71},{8,72},{9,... | collective-permute-start | bytes 3145736 | tf_op jit(solution)/shard_map/ppermute | solution.py:29
  52.3 7.0 %collective-permute-start.8 = (bf16[112,1024]{1,0:T(8,128)(2,1)S(1)}, bf16[112,1024]{1,0:T(8,128)(2,1)}, u32[]{:S(2)}, u32[]{:S(2)}) collective-permute-start(bf16[112,1024]{1,0:T(8,128)(2,1)S(1)} %collective-permute-done.4.refs_2_), channel_id=1, source_target_pairs={{0,8},{1,9},{2,10},{3,11},{4,12},{5,13},{6,14},{7,15},{8,16},{9,17... | collective-permute-start | bytes 688136 | tf_op jit(solution)/shard_map/ppermute | solution.py:29
  54.6 7.8 %collective-permute-start.10 = (bf16[112,1024]{1,0:T(8,128)(2,1)S(1)}, bf16[112,1024]{1,0:T(8,128)(2,1)}, u32[]{:S(2)}, u32[]{:S(2)}) collective-permute-start(bf16[112,1024]{1,0:T(8,128)(2,1)S(1)} %collective-permute-done.6.refs_6_), channel_id=1, source_target_pairs={{0,56},{1,57},{2,58},{3,59},{4,60},{5,61},{6,62},{7,63},{8,0},{9,1... | collective-permute-start | bytes 688136 | tf_op jit(solution)/shard_map/ppermute | solution.py:29
  59.3 6.2 %collective-permute-start.9 = (bf16[112,1024]{1,0:T(8,128)(2,1)}, bf16[112,1024]{1,0:T(8,128)(2,1)}, u32[]{:S(2)}, u32[]{:S(2)}) collective-permute-start(bf16[112,1024]{1,0:T(8,128)(2,1)} %collective-permute-done.8.refs_3_), channel_id=1, source_target_pairs={{0,8},{1,9},{2,10},{3,11},{4,12},{5,13},{6,14},{7,15},{8,16},{9,17... | collective-permute-start | bytes 688136 | tf_op jit(solution)/shard_map/ppermute | solution.py:29
  78.0 8.4 %collective-permute-start.17 = (bf16[512,1024]{1,0:T(8,128)(2,1)S(1)}, bf16[512,1024]{1,0:T(8,128)(2,1)S(1)}, u32[]{:S(2)}, u32[]{:S(2)}) collective-permute-start(bf16[512,1024]{1,0:T(8,128)(2,1)S(1)} %collective-permute-done.13.refs_8_), channel_id=1, source_target_pairs={{0,1},{1,0},{2,3},{3,2},{4,5},{5,4},{6,7},{7,6},{8,9},{9,8},{10,11... | collective-permute-start | bytes 3145736 | tf_op jit(solution)/shard_map/ppermute | solution.py:29
  79.3 13.0 %copy-start.28 = (s32[4]{0:T(128)}, s32[4]{0:T(128)S(1)}, u32[]{:S(2)}) copy-start(s32[4]{0:T(128)S(1)} %get-tuple-element.76.xs) | copy-start | bytes 52
  79.6 13.4 %collective-permute-start.14 = (bf16[112,1536]{1,0:T(8,128)(2,1)}, bf16[112,1536]{1,0:T(8,128)(2,1)S(1)}, u32[]{:S(2)}, u32[]{:S(2)}) collective-permute-start(bf16[112,1536]{1,0:T(8,128)(2,1)} %get-tuple-element.55), channel_id=1, source_target_pairs={{0,4},{1,5},{2,6},{3,7},{4,0},{5,1},{6,2},{7,3},{8,12},{9,13},{10,... | collective-permute-start | bytes 1032200 | tf_op jit(solution)/shard_map/ppermute | solution.py:29
  82.6 16.4 %collective-permute-start.15 = (bf16[112,1536]{1,0:T(8,128)(2,1)}, bf16[112,1536]{1,0:T(8,128)(2,1)S(1)}, u32[]{:S(2)}, u32[]{:S(2)}) collective-permute-start(bf16[112,1536]{1,0:T(8,128)(2,1)} %get-tuple-element.56), channel_id=1, source_target_pairs={{0,2},{1,3},{2,4},{3,5},{4,6},{5,7},{6,0},{7,1},{8,10},{9,11},{10,... | collective-permute-start | bytes 1032200 | tf_op jit(solution)/shard_map/ppermute | solution.py:29
  83.1 15.9 %collective-permute-start.16 = (bf16[112,1536]{1,0:T(8,128)(2,1)}, bf16[112,1536]{1,0:T(8,128)(2,1)S(1)}, u32[]{:S(2)}, u32[]{:S(2)}) collective-permute-start(bf16[112,1536]{1,0:T(8,128)(2,1)} %get-tuple-element.57), channel_id=1, source_target_pairs={{0,6},{1,7},{2,0},{3,1},{4,2},{5,3},{6,4},{7,5},{8,14},{9,15},{10,... | collective-permute-start | bytes 1032200 | tf_op jit(solution)/shard_map/ppermute | solution.py:29
  92.3 8.6 %collective-permute-start.18 = (bf16[112,512]{1,0:T(8,128)(2,1)}, bf16[112,512]{1,0:T(8,128)(2,1)S(1)}, u32[]{:S(2)}, u32[]{:S(2)}) collective-permute-start(bf16[112,512]{1,0:T(8,128)(2,1)} %get-tuple-element.60), channel_id=1, source_target_pairs={{0,4},{1,5},{2,6},{3,7},{4,0},{5,1},{6,2},{7,3},{8,12},{9,13},{10,... | collective-permute-start | bytes 344072 | tf_op jit(solution)/shard_map/ppermute | solution.py:29
  92.4 11.2 %collective-permute-start.19 = (bf16[112,512]{1,0:T(8,128)(2,1)}, bf16[112,512]{1,0:T(8,128)(2,1)S(1)}, u32[]{:S(2)}, u32[]{:S(2)}) collective-permute-start(bf16[112,512]{1,0:T(8,128)(2,1)} %get-tuple-element.61), channel_id=1, source_target_pairs={{0,2},{1,3},{2,4},{3,5},{4,6},{5,7},{6,0},{7,1},{8,10},{9,11},{10,... | collective-permute-start | bytes 344072 | tf_op jit(solution)/shard_map/ppermute | solution.py:29
  93.0 10.8 %copy-start.15 = (bf16[112,1536]{1,0:T(8,128)(2,1)}, bf16[112,1536]{1,0:T(8,128)(2,1)S(1)}, u32[]{:S(2)}) copy-start(bf16[112,1536]{1,0:T(8,128)(2,1)S(1)} %collective-permute-done.14.refs_1_) | copy-start | bytes 1032196
  93.0 10.8 %collective-permute-start.20 = (bf16[112,512]{1,0:T(8,128)(2,1)}, bf16[112,512]{1,0:T(8,128)(2,1)S(1)}, u32[]{:S(2)}, u32[]{:S(2)}) collective-permute-start(bf16[112,512]{1,0:T(8,128)(2,1)} %get-tuple-element.62), channel_id=1, source_target_pairs={{0,6},{1,7},{2,0},{3,1},{4,2},{5,3},{6,4},{7,5},{8,14},{9,15},{10,... | collective-permute-start | bytes 344072 | tf_op jit(solution)/shard_map/ppermute | solution.py:29
  104.4 11.1 %copy-start.29 = (bf16[448]{0:T(512)(128)(2,1)S(1)}, bf16[448]{0:T(512)(128)(2,1)}, u32[]{:S(2)}) copy-start(bf16[448]{0:T(512)(128)(2,1)} %param.21) | copy-start | bytes 2692
  104.4 11.1 %copy-start.30 = (bf16[448]{0:T(512)(128)(2,1)S(1)}, bf16[448]{0:T(512)(128)(2,1)}, u32[]{:S(2)}) copy-start(bf16[448]{0:T(512)(128)(2,1)} %param.22) | copy-start | bytes 2692
  108.6 8.5 %copy-start.4 = (bf16[512,896]{1,0:T(8,128)(2,1)S(1)}, bf16[512,896]{1,0:T(8,128)(2,1)}, u32[]{:S(2)}) copy-start(bf16[512,896]{1,0:T(8,128)(2,1)} %param.23) | copy-start | bytes 2752516
  108.6 8.5 %copy-start.5 = (bf16[512,896]{1,0:T(8,128)(2,1)S(1)}, bf16[512,896]{1,0:T(8,128)(2,1)}, u32[]{:S(2)}) copy-start(bf16[512,896]{1,0:T(8,128)(2,1)} %param.24) | copy-start | bytes 2752516
  108.6 41.5 %all-to-all-start = ((bf16[32,112,128]{2,1,0:T(8,128)(2,1)}), bf16[32,112,128]{2,1,0:T(8,128)(2,1)S(1)}, u32[]{:S(2)}, u32[]{:S(2)}) async-start(bf16[32,112,128]{2,1,0:T(8,128)(2,1)} %send.1), calls=%async_computation | async-start | bytes 1835008 | tf_op jit(solution)/shard_map/all_to_all | solution.py:366
  127.9 52.7 %copy-start.31 = (s32[8]{0:T(128)S(1)}, s32[8]{0:T(128)}, u32[]{:S(2)}) copy-start(s32[8]{0:T(128)} %constant.211.clone) | copy-start | bytes 100
  154.4 11.6 %collective-permute-start.22 = (bf16[464,512]{1,0:T(8,128)(2,1)}, bf16[464,512]{1,0:T(8,128)(2,1)S(1)}, u32[]{:S(2)}, u32[]{:S(2)}) collective-permute-start(bf16[464,512]{1,0:T(8,128)(2,1)} %recv.1.refs_0_), channel_id=1, source_target_pairs={{0,2},{1,3},{2,4},{3,5},{4,6},{5,7},{6,0},{7,1},{8,10},{9,11},{10,... | collective-permute-start | bytes 1425416 | tf_op jit(solution)/shard_map/ppermute | solution.py:29
  155.6 14.8 %collective-permute-start.24 = (bf16[464,512]{1,0:T(8,128)(2,1)}, bf16[464,512]{1,0:T(8,128)(2,1)S(1)}, u32[]{:S(2)}, u32[]{:S(2)}) collective-permute-start(bf16[464,512]{1,0:T(8,128)(2,1)} %recv.1.refs_0_), channel_id=1, source_target_pairs={{0,6},{1,7},{2,0},{3,1},{4,2},{5,3},{6,4},{7,5},{8,14},{9,15},{10,... | collective-permute-start | bytes 1425416 | tf_op jit(solution)/shard_map/ppermute | solution.py:29
  157.1 21.6 %collective-permute-start.26 = (bf16[464,512]{1,0:T(8,128)(2,1)}, bf16[464,512]{1,0:T(8,128)(2,1)S(1)}, u32[]{:S(2)}, u32[]{:S(2)}) collective-permute-start(bf16[464,512]{1,0:T(8,128)(2,1)} %recv.1.refs_0_), channel_id=1, source_target_pairs={{0,4},{1,5},{2,6},{3,7},{4,0},{5,1},{6,2},{7,3},{8,12},{9,13},{10,... | collective-permute-start | bytes 1425416 | tf_op jit(solution)/shard_map/ppermute | solution.py:29
  158.3 22.9 %collective-permute-start.21 = (bf16[464,512]{1,0:T(8,128)(2,1)}, bf16[464,512]{1,0:T(8,128)(2,1)S(1)}, u32[]{:S(2)}, u32[]{:S(2)}) collective-permute-start(bf16[464,512]{1,0:T(8,128)(2,1)} %recv.1.refs_0_), channel_id=1, source_target_pairs={{0,1},{1,0},{2,3},{3,2},{4,5},{5,4},{6,7},{7,6},{8,9},{9,8},{10,11... | collective-permute-start | bytes 1425416 | tf_op jit(solution)/shard_map/ppermute | solution.py:29
  166.0 15.9 %copy-start.8 = (bf16[464,512]{1,0:T(8,128)(2,1)}, bf16[464,512]{1,0:T(8,128)(2,1)S(1)}, u32[]{:S(2)}) copy-start(bf16[464,512]{1,0:T(8,128)(2,1)S(1)} %collective-permute-done.22.refs_2_) | copy-start | bytes 1425412
  166.0 15.2 %collective-permute-start.23 = (bf16[464,512]{1,0:T(8,128)(2,1)S(1)}, bf16[464,512]{1,0:T(8,128)(2,1)S(1)}, u32[]{:S(2)}, u32[]{:S(2)}) collective-permute-start(bf16[464,512]{1,0:T(8,128)(2,1)S(1)} %collective-permute-done.22.refs_2_), channel_id=1, source_target_pairs={{0,1},{1,0},{2,3},{3,2},{4,5},{5,4},{6,7},{7,6},{8,9},{9,8},{10,11... | collective-permute-start | bytes 1425416 | tf_op jit(solution)/shard_map/ppermute | solution.py:29
  170.4 11.6 %copy-start.9 = (bf16[464,512]{1,0:T(8,128)(2,1)}, bf16[464,512]{1,0:T(8,128)(2,1)S(1)}, u32[]{:S(2)}) copy-start(bf16[464,512]{1,0:T(8,128)(2,1)S(1)} %collective-permute-done.24.refs_4_) | copy-start | bytes 1425412
  170.4 10.9 %collective-permute-start.25 = (bf16[464,512]{1,0:T(8,128)(2,1)S(1)}, bf16[464,512]{1,0:T(8,128)(2,1)S(1)}, u32[]{:S(2)}, u32[]{:S(2)}) collective-permute-start(bf16[464,512]{1,0:T(8,128)(2,1)S(1)} %collective-permute-done.24.refs_4_), channel_id=1, source_target_pairs={{0,1},{1,0},{2,3},{3,2},{4,5},{5,4},{6,7},{7,6},{8,9},{9,8},{10,11... | collective-permute-start | bytes 1425416 | tf_op jit(solution)/shard_map/ppermute | solution.py:29
  178.7 3.2 %collective-permute-start.27 = (bf16[464,512]{1,0:T(8,128)(2,1)S(1)}, bf16[464,512]{1,0:T(8,128)(2,1)S(1)}, u32[]{:S(2)}, u32[]{:S(2)}) collective-permute-start(bf16[464,512]{1,0:T(8,128)(2,1)S(1)} %collective-permute-done.26.refs_6_), channel_id=1, source_target_pairs={{0,1},{1,0},{2,3},{3,2},{4,5},{5,4},{6,7},{7,6},{8,9},{9,8},{10,11... | collective-permute-start | bytes 1425416 | tf_op jit(solution)/shard_map/ppermute | solution.py:29
  (18 other events, 44.0 us)
Sparse Core Ops, SparseCore 0:
  11.0 51.4 all-gather.2
  65.1 102.6 all-gather.4
